TPU v7x, 256 devices: a whole 4x4x8 slice. The times are simulated.
256 devices in a mesh: dp: 32 (over x, z_hi, core), head: 8 (over z_lo, y).
Axes of the slice: x: 4, y: 4, z: 8 (z_hi: 4, z_lo: 2; z = z_hi * 2 + z_lo), core: 2. Of those that a mesh axis runs over, the one named last changes fastest.
Arguments:
- q_nope: bfloat16 [256, 4, 16384], P('dp', None, 'head'), may hold values from -120 to 120
- q_rope: bfloat16 [256, 4, 8192], P('dp', None, 'head'), may hold values from -6 to 6
- new_latent: bfloat16 [256, 4, 512], P('dp'), may hold values from -6 to 6
- new_rope: bfloat16 [256, 4, 64], P('dp'), may hold values from -6 to 6
- pool_latent: bfloat16 [2048, 64, 512], P('dp', 'head'), may hold values from -6 to 6
- pool_rope: bfloat16 [2048, 4096], P('dp', 'head'), may hold values from -6 to 6
- kv_weight: bfloat16 [512, 128, 256], P('dp', 'head'), may hold values from -0.25 to 0.25
- src_dev: int32 [4096, 1], P('dp'), may hold values from 0 to 31; in each aligned block of 128 rows (0 to 127, 128 to 255, ...) at most 5 rows name the same one
- src_block: int32 [4096], P('dp'), may hold values from 0 to 63
- lengths: int32 [256], P('dp'), may hold values from 1 to 1024
Outputs:
- attn_out: bfloat16 [256, 4, 16384], P('dp', None, 'head')
Inputs may be any that keep to these rules, and one draw needn't show every extreme that they name: `src_dev`: among the 128 table entries of one index of dp, at most 5 name the same index of dp, a bound that some block reaches.
All inputs are finite; a program needn't handle non-finite values.
Results may differ from a plain program's by a relative error of at most 0.006.
The roundings to bfloat16 on the way count: a program that leaves them out, or rounds other values in their place, can miss the bound.
Values may be sent and summed in bfloat16 or wider, within the bound.
A program may use at most 128 MiB of HBM per device.

v0:
```python
import jax
import jax.numpy as jnp
from jax import lax
from jax.sharding import PartitionSpec as P

LAT = 512
ROPE = 64
NOPE = 128
DV = 128


def rotate(values, positions):
    half = values.shape[-1] // 2
    freqs = 10000.0 ** (-(2.0 * jnp.arange(half, dtype=jnp.float32)) / (2.0 * half))
    angles = positions[..., None] * freqs
    first = values[..., :half]
    second = values[..., half:]
    cosine = jnp.cos(angles)
    sine = jnp.sin(angles)
    return jnp.concatenate(
        [first * cosine - second * sine, first * sine + second * cosine], axis=-1
    )


def per_device(
    q_nope,
    q_rope,
    new_latent,
    new_rope,
    pool_latent,
    pool_rope,
    kv_weight,
    src_dev,
    src_block,
    lengths,
):
    dp_count = lax.axis_size("dp")
    weights = lax.all_gather(kv_weight, "dp", axis=0, tiled=True)
    groups = weights.shape[1]
    w_key = weights[:, :, :NOPE]
    w_val = weights[:, :, NOPE:]
    requests = lengths.shape[0]
    entries = src_block.shape[0]
    steps = q_nope.shape[1]
    capacity = max(2, 5 * entries // (4 * dp_count))
    scale = (NOPE + ROPE) ** (-0.5)
    all_dev, all_blocks = (
        lax.all_gather(src_dev, "dp", axis=0, tiled=True),
        lax.all_gather(src_block, "dp", axis=0, tiled=True),
    )
    own_index = lax.axis_index("dp")
    dev_table = all_dev[:, 0].reshape(dp_count, entries)
    block_table = all_blocks.reshape(dp_count, entries)
    matches = (dev_table == own_index).astype(jnp.int32)
    ranking = jnp.cumsum(matches, axis=1) - 1
    slot_ids = jnp.arange(capacity, dtype=jnp.int32)
    chosen = (matches[:, None, :] == 1) & (ranking[:, None, :] == slot_ids[None, :, None])
    picked = jnp.sum(jnp.where(chosen, block_table[:, None, :], 0), axis=2)
    send_lat = pool_latent[picked]
    send_rope = pool_rope[picked]
    full_lat, full_rope = (
        lax.all_gather(send_lat, "head", axis=2, tiled=True),
        lax.all_gather(send_rope, "head", axis=2, tiled=True),
    )
    recv_lat, recv_rope = (
        lax.all_to_all(full_lat, "dp", split_axis=0, concat_axis=0, tiled=True),
        lax.all_to_all(full_rope, "dp", split_axis=0, concat_axis=0, tiled=True),
    )
    block_len = recv_lat.shape[2]
    own_dev = src_dev[:, 0]
    onehot = (own_dev[:, None] == jnp.arange(dp_count, dtype=jnp.int32)[None, :]).astype(jnp.int32)
    before = jnp.cumsum(onehot, axis=0) - onehot
    arrival = jnp.sum(before * onehot, axis=1)
    slot_index = own_dev * capacity + arrival
    cache_lat = recv_lat.reshape(dp_count * capacity, block_len, LAT)[slot_index].reshape(
        requests, -1, LAT
    )
    cache_rope = recv_rope.reshape(dp_count * capacity, block_len * ROPE)[slot_index].reshape(
        requests, -1, ROPE
    )
    tokens = cache_lat.shape[1]
    query_n = q_nope.reshape(requests, steps, groups, NOPE)
    q_lat = jnp.einsum("rshn,lhn->rshl", query_n, w_key, preferred_element_type=jnp.float32).astype(
        jnp.bfloat16
    )
    positions = (lengths[:, None] + jnp.arange(steps, dtype=jnp.int32)[None, :]).astype(jnp.float32)
    q_rot = rotate(
        q_rope.reshape(requests, steps, groups, ROPE).astype(jnp.float32), positions[:, :, None]
    ).astype(jnp.bfloat16)
    k_new = rotate(new_rope.astype(jnp.float32), positions).astype(jnp.bfloat16)
    queries = q_lat.reshape(requests, steps * groups, LAT)
    rotated = q_rot.reshape(requests, steps * groups, ROPE)
    cached = jnp.einsum("rql,rtl->rqt", queries, cache_lat, preferred_element_type=jnp.float32)
    cached = cached + jnp.einsum(
        "rqe,rte->rqt", rotated, cache_rope, preferred_element_type=jnp.float32
    )
    fresh = jnp.einsum("rql,rul->rqu", queries, new_latent, preferred_element_type=jnp.float32)
    fresh = fresh + jnp.einsum("rqe,rue->rqu", rotated, k_new, preferred_element_type=jnp.float32)
    scores = jnp.concatenate([cached, fresh], axis=-1) * scale
    token_ids = jnp.arange(tokens, dtype=jnp.int32)
    valid_old = jnp.broadcast_to(
        (token_ids[None, :] < lengths[:, None])[:, None, :], (requests, steps * groups, tokens)
    )
    step_of_row = jnp.arange(steps * groups, dtype=jnp.int32) // groups
    valid_new = jnp.arange(steps, dtype=jnp.int32)[None, :] <= step_of_row[:, None]
    valid_new = jnp.broadcast_to(valid_new[None, :, :], (requests, steps * groups, steps))
    valid = jnp.concatenate([valid_old, valid_new], axis=-1)
    probs = jax.nn.softmax(jnp.where(valid, scores, -jnp.inf), axis=-1).astype(jnp.bfloat16)
    o_lat = jnp.einsum(
        "rqt,rtl->rql", probs[..., :tokens], cache_lat, preferred_element_type=jnp.float32
    )
    o_lat = o_lat + jnp.einsum(
        "rqu,rul->rql", probs[..., tokens:], new_latent, preferred_element_type=jnp.float32
    )
    o_lat = o_lat.astype(jnp.bfloat16).reshape(requests, steps, groups, LAT)
    result = jnp.einsum("rshl,lhv->rshv", o_lat, w_val, preferred_element_type=jnp.float32).astype(
        jnp.bfloat16
    )
    return result.reshape(requests, steps, groups * DV)


def solution(mesh):
    in_specs = (
        P("dp", None, "head"),
        P("dp", None, "head"),
        P("dp", None, None),
        P("dp", None, None),
        P("dp", "head", None),
        P("dp", "head"),
        P("dp", "head", None),
        P("dp", None),
        P("dp"),
        P("dp"),
    )
    out_specs = P("dp", None, "head")
    return jax.shard_map(
        per_device, mesh=mesh, in_specs=in_specs, out_specs=out_specs, check_vma=False
    )
```

profile of v0, /device:TPU:1, one launch (start us, length us, event | category | flops | bytes accessed | tf_op | source)
XLA Modules:
  0.0 587.4 jit_solution(5982721753619983224)
XLA Ops:
  7.4 48.7 %all_gather.16 = s32[4096,1]{0,1:T(1,128)S(1)} all-gather(s32[128,1]{0,1:T(1,128)} %param.17), channel_id=1, replica_groups=mesh['dp'=32,'head'=8] {'dp'}, dimensions={0}, use_global_device_ids=true | all-gather | bytes 16896 | tf_op jit(solution)/shard_map/all_gather | solution.py:48
  56.4 39.1 %all-gather.2 = s32[32,1,128]{2,1,0:T(1,128)S(1)} all-gather(s32[1,1,128]{2,1,0:T(1,128)} %bitcast.69), channel_id=1, replica_groups=mesh['dp'=32,'head'=8] {'dp'}, dimensions={0}, use_global_device_ids=true | all-gather | bytes 16896 | tf_op jit(solution)/shard_map/all_gather | solution.py:49
  95.8 1.8 gather_fusion.2
  97.6 0.8 reshape.217
  98.5 2.0 gather_fusion
  100.5 33.2 %all-gather.11.cloned.1.call-done = bf16[32,5,4096]{2,1,0:T(8,128)(2,1)} async-done(((bf16[32,5,512]{2,1,0:T(8,128)(2,1)}), bf16[32,5,4096]{2,1,0:T(8,128)(2,1)}) %all-gather.11.cloned.1.call-update) | async-done | bytes 1310736 | tf_op jit(solution)/shard_map/all_gather | solution.py:63
  133.8 86.9 %all_to_all.10 = bf16[32,5,4096]{2,1,0:T(8,128)(2,1)} all-to-all(bf16[32,5,4096]{2,1,0:T(8,128)(2,1)} %all-gather.11.cloned.1.call-done), channel_id=1, replica_groups=mesh['dp'=32,'head'=8] {'dp'}, dimensions={0} | all-to-all | bytes 2621440 | tf_op jit(solution)/shard_map/all_to_all | solution.py:67
  220.7 73.5 %all-gather.9.cloned.1.call-done = bf16[32,5,64,512]{3,2,1,0:T(8,128)(2,1)} async-done(((bf16[32,5,8,512]{3,2,1,0:T(8,128)(2,1)}), bf16[32,5,64,512]{3,2,1,0:T(8,128)(2,1)}) %all-gather.9.cloned.1.call-update) | async-done | bytes 10485776 | tf_op jit(solution)/shard_map/all_gather | solution.py:62
  294.3 9.8 %all-to-all-start = ((bf16[32,5,64,512]{3,2,1,0:T(8,128)(2,1)}), bf16[32,5,64,512]{3,2,1,0:T(8,128)(2,1)}, u32[]{:S(2)}, u32[]{:S(2)}) async-start(bf16[32,5,64,512]{3,2,1,0:T(8,128)(2,1)} %all-gather.9.cloned.1.call-done), calls=%async_computation | async-start | bytes 20971520 | tf_op jit(solution)/shard_map/all_to_all | solution.py:66
  304.3 0.7 copy.49
  306.7 1.8 reshape.190
  308.5 2.3 gather_fusion.3
  310.8 3.3 reshape.191
  314.1 238.2 %all-gather.7.cloned.1.call-done = bf16[512,16,256]{2,0,1:T(8,128)(2,1)} async-done(((bf16[16,16,256]{2,0,1:T(8,128)(2,1)}), bf16[512,16,256]{2,0,1:T(8,128)(2,1)}) %all-gather.7.cloned.1.call-update) | async-done | bytes 4194320 | tf_op jit(solution)/shard_map/all_gather | solution.py:38
  552.3 2.4 fusion.10
  555.2 0.9 copy.56
  556.2 10.6 %gather_fusion.1 = bf16[128,64,512]{2,1,0:T(8,128)(2,1)} fusion(bf16[160,64,512]{2,1,0:T(8,128)(2,1)} %bitcast.9, s32[1024]{0:T(1024)S(1)} %pad_clamp_fusion), kind=kCustom, calls=%fused_computation.1 | custom fusion | bytes 16777728 | tf_op jit(solution)/shard_map/gather | solution.py:75
  566.7 6.0 %fusion.33 = f32[8,64,1024]{2,1,0:T(8,128)S(1)} fusion(bf16[8,64,512]{2,1,0:T(8,128)(2,1)S(1)} %bitcast.58, bf16[8,1024,512]{2,1,0:T(8,128)(2,1)} %bitcast.52), kind=kOutput, calls=%fused_computation.70 | convolution fusion | flops 536870912 | bytes 11010048 | tf_op jit(solution)/shard_map/rql,rtl->rqt/dot_general | solution.py:93
  572.7 0.9 convolution_add_fusion
  573.8 1.8 fusion.32
  576.0 0.5 slice-done.1
  576.5 1.5 fusion.15
  578.7 0.5 fusion.14
  579.3 0.7 reshape.237
  (64 shorter events, 4.3 us)
Async XLA Ops:
  7.4 91.1 %copy-start = (bf16[64,8,512]{2,1,0:T(8,128)(2,1)S(1)}, bf16[64,8,512]{2,1,0:T(8,128)(2,1)}, u32[]{:S(2)}) copy-start(bf16[64,8,512]{2,1,0:T(8,128)(2,1)} %param.14) | copy-start | bytes 1572868
  7.4 126.4 %all-gather.11.cloned.1.call-start = ((), (), s32[]{:S(2)}) async-start(), calls=%async_computation.4 | async-start | bytes 2359296 | tf_op jit(solution)/shard_map/all_gather | solution.py:63
  98.5 195.8 %all-gather.9.cloned.1.call-start = ((), (), s32[]{:S(2)}) async-start(), calls=%async_computation.3 | async-start | bytes 11796480 | tf_op jit(solution)/shard_map/all_gather | solution.py:62
  220.7 83.6 %copy-start.3 = (bf16[16,16,256]{2,1,0:T(8,128)(2,1)S(1)}, bf16[16,16,256]{2,1,0:T(8,128)(2,1)}, u32[]{:S(2)}) copy-start(bf16[16,16,256]{2,1,0:T(8,128)(2,1)} %param.16) | copy-start | bytes 393220
  220.7 84.3 %copy-start.7 = (s32[128,1]{0,1:T(1,128)S(1)}, s32[128,1]{0,1:T(1,128)}, u32[]{:S(2)}) copy-start(s32[128,1]{0,1:T(1,128)} %param.17) | copy-start | bytes 1540
  220.7 84.6 %copy-start.4 = (bf16[8,4,2048]{2,1,0:T(4,128)(2,1)S(1)}, bf16[8,4,2048]{2,1,0:T(4,128)(2,1)}, u32[]{:S(2)}) copy-start(bf16[8,4,2048]{2,1,0:T(4,128)(2,1)} %param.10) | copy-start | bytes 393220
  220.7 84.7 %copy-start.6 = (bf16[8,4,64]{2,1,0:T(4,128)(2,1)S(1)}, bf16[8,4,64]{2,1,0:T(4,128)(2,1)}, u32[]{:S(2)}) copy-start(bf16[8,4,64]{2,1,0:T(4,128)(2,1)} %param.13) | copy-start | bytes 12292
  220.7 84.7 %copy-start.5 = (bf16[8,4,1024]{2,1,0:T(4,128)(2,1)S(1)}, bf16[8,4,1024]{2,1,0:T(4,128)(2,1)}, u32[]{:S(2)}) copy-start(bf16[8,4,1024]{2,1,0:T(4,128)(2,1)} %param.11) | copy-start | bytes 196612
  220.7 85.1 %copy-start.8 = (s32[8]{0:T(128)S(1)}, s32[8]{0:T(128)}, u32[]{:S(2)}) copy-start(s32[8]{0:T(128)} %param.19) | copy-start | bytes 100
  294.3 261.9 %all-to-all-start = ((bf16[32,5,64,512]{3,2,1,0:T(8,128)(2,1)}), bf16[32,5,64,512]{3,2,1,0:T(8,128)(2,1)}, u32[]{:S(2)}, u32[]{:S(2)}) async-start(bf16[32,5,64,512]{3,2,1,0:T(8,128)(2,1)} %all-gather.9.cloned.1.call-done), calls=%async_computation | async-start | bytes 20971520 | tf_op jit(solution)/shard_map/all_to_all | solution.py:66
  304.1 248.2 %all-gather.7.cloned.1.call-start = ((), (), s32[]{:S(2)}) async-start(), calls=%async_computation.2 | async-start | bytes 4325376 | tf_op jit(solution)/shard_map/all_gather | solution.py:38
  314.0 240.9 %copy-start.2 = (bf16[8,4,512]{2,1,0:T(4,128)(2,1)S(1)}, bf16[8,4,512]{2,1,0:T(4,128)(2,1)}, u32[]{:S(2)}) copy-start(bf16[8,4,512]{2,1,0:T(4,128)(2,1)} %param.12) | copy-start | bytes 98308
  572.7 1.1 copy-start.1
  572.7 3.3 slice-start
  573.8 2.7 slice-start.1
  576.5 2.2 copy-start.9
Sparse Core Ops, SparseCore 0:
  98.6 35.1 all-gather.10
  135.5 158.6 all-gather.8
Sparse Core Ops, SparseCore 1:
  307.0 245.2 all-gather.6
where the time goes:
time: 598 us; the launch traced here: 587 us
  waiting for transfers between devices  345 us (58%)
  blocking collectives  175 us (29%)
  local copies, waits for them, and re-layouts  26.6 us (4%)
  between operations  15.2 us (3%)
  matrix products  12.1 us (2%)
  starting transfers between devices  10.1 us (2%)
    all_gather x1, waiting for transfers between devices, per_device(): weights = lax.all_gather(kv_weight, 'dp', axis=0, tiled=True)  238 us
    all_to_all x1, blocking collectives, per_device(): lax.all_to_all(full_rope, 'dp', split_axis=0, concat_axis=0, tiled=True)  86.9 us
    all_gather x1, waiting for transfers between devices, per_device(): lax.all_gather(send_lat, 'head', axis=2, tiled=True)  73.5 us
    all_gather x1, blocking collectives, per_device(): lax.all_gather(src_dev, 'dp', axis=0, tiled=True)  48.7 us
    all_gather x1, blocking collectives, per_device(): lax.all_gather(src_block, 'dp', axis=0, tiled=True)  39.1 us
    all_gather x1, waiting for transfers between devices, per_device(): lax.all_gather(send_rope, 'head', axis=2, tiled=True)  33.2 us
  transfers between devices with their start and end apart: 4, of which 3 were waited for; matrix products, arithmetic and copies ran while one was open for 3% of the time, Pallas kernels for 0%

commit v1 on v0

v1 whole, which is shorter than its diff:
```python
import jax
import jax.numpy as jnp
from jax import lax
from jax.experimental import pallas as pl
from jax.experimental.pallas import tpu as pltpu
from jax.sharding import PartitionSpec as P

LAT = 512
ROPE = 64
NOPE = 128
DV = 128
CAP = 5
NDP = 32
NH = 8
MESH = pl.DeviceIdType.MESH
F32 = jnp.float32
BF16 = jnp.bfloat16
SCALE = (NOPE + ROPE) ** (-0.5)


def rotate(values, positions):
    half = values.shape[-1] // 2
    freqs = 10000.0 ** (-(2.0 * jnp.arange(half, dtype=jnp.float32)) / (2.0 * half))
    angles = positions[..., None] * freqs
    first = values[..., :half]
    second = values[..., half:]
    cosine = jnp.cos(angles)
    sine = jnp.sin(angles)
    return jnp.concatenate(
        [first * cosine - second * sine, first * sine + second * cosine], axis=-1
    )


def remote(src, dst, send_sem, recv_sem, device):
    return pltpu.make_async_remote_copy(
        src_ref=src,
        dst_ref=dst,
        send_sem=send_sem,
        recv_sem=recv_sem,
        device_id=device,
        device_id_type=MESH,
    )


def dot_nt(a, b):
    return lax.dot_general(a, b, (((1,), (1,)), ((), ())), preferred_element_type=F32)


def dot_nn(a, b):
    return lax.dot_general(a, b, (((1,), (0,)), ((), ())), preferred_element_type=F32)


def kernel(
    req_ref, slot_ref, rtab_ref, len_ref, pool_ref, rope_ref, wk_ref, wv_ref, qn_ref, qr_ref,
    newl_ref, newr_ref, out_ref,
    reqv, reqs, slat, srope, rlat, rrope, rropef, clat, crope, kmat, kr, wkf, wvf,
    qsend, qmat, qrm, osend, oall,
    local_sem, req_ss, req_rs, lat_ss, lat_rs, rope_ss, rope_rs,
    wk_ss, wk_rs, wv_ss, wv_rs, q_ss, q_rs, qr_ss, qr_rs, c_ss, c_rs, cr_ss, cr_rs, o_ss, o_rs,
):
    me = lax.axis_index("dp")
    h = lax.axis_index("head")
    x, zh, c = me // 8, (me // 2) % 4, me % 2

    def dp_peer(o):
        return ((x + o // 8) % 4) * 8 + ((zh + (o // 2) % 4) % 4) * 2 + (c + o % 2) % 2

    def head_peer(k):
        return (h + k) % NH

    barrier = pltpu.get_barrier_semaphore()

    @pl.loop(1, NDP)
    def _(o):
        pl.semaphore_signal(barrier, inc=1, device_id=(dp_peer(o), h), device_id_type=MESH)

    @pl.loop(1, NH)
    def _(k):
        pl.semaphore_signal(barrier, inc=1, device_id=(me, head_peer(k)), device_id_type=MESH)

    pl.semaphore_wait(barrier, NDP - 1 + NH - 1)

    def req_copy(o):
        p = dp_peer(o)
        return remote(req_ref.at[p], reqv.at[me], req_ss.at[p], req_rs.at[me], (p, h))

    def req_arrival(o):
        p = dp_peer(o)
        return remote(req_ref.at[p], reqv.at[p], req_ss.at[p], req_rs.at[p], (p, h))

    @pl.loop(1, NDP)
    def _(o):
        req_copy(o).start()

    def z_copy(own, full, ss, rs, k):
        p = (x * 8 + ((zh + k) % 4) * 2 + c, h)
        return remote(own, full.at[x, zh, c], ss.at[k], rs.at[k], p)

    def z_arrival(own, full, ss, rs, k):
        z = (zh + 4 - k) % 4
        return remote(own, full.at[x, z, c], ss.at[k], rs.at[k], (x * 8 + z * 2 + c, h))

    def x_copy(full, ss, rs, k):
        p = (((x + k) % 4) * 8 + zh * 2 + c, h)
        return remote(full.at[x, :, c], full.at[x, :, c], ss.at[3 + k], rs.at[3 + k], p)

    def x_arrival(full, ss, rs, k):
        xx = (x + 4 - k) % 4
        return remote(
            full.at[xx, :, c], full.at[xx, :, c], ss.at[3 + k], rs.at[3 + k], (xx * 8 + zh * 2 + c, h)
        )

    def core_copy(full, ss, rs):
        p = (x * 8 + zh * 2 + (1 - c), h)
        return remote(full.at[:, :, c], full.at[:, :, c], ss.at[7], rs.at[7], p)

    def core_arrival(full, ss, rs):
        p = (x * 8 + zh * 2 + (1 - c), h)
        return remote(full.at[:, :, 1 - c], full.at[:, :, 1 - c], ss.at[7], rs.at[7], p)

    def z_stage(own, full, ss, rs, sem):
        pltpu.make_async_copy(own, full.at[x, zh, c], sem).start()
        for k in (1, 2, 3):
            z_copy(own, full, ss, rs, k).start()

    def x_stage(own, full, ss, rs, sem):
        pltpu.make_async_copy(own, full.at[x, zh, c], sem).wait()
        for k in (1, 2, 3):
            z_arrival(own, full, ss, rs, k).wait_recv()
        for k in (1, 2, 3):
            x_copy(full, ss, rs, k).start()

    def core_stage(full, ss, rs):
        for k in (1, 2, 3):
            x_arrival(full, ss, rs, k).wait_recv()
        core_copy(full, ss, rs).start()

    def weights_sent(own, full, ss, rs):
        for k in (1, 2, 3):
            z_copy(own, full, ss, rs, k).wait_send()
            x_copy(full, ss, rs, k).wait_send()
        core_copy(full, ss, rs).wait_send()

    z_stage(wk_ref, wkf, wk_ss, wk_rs, local_sem.at[0])

    reqv[pl.ds(me, 1)] = req_ref[pl.ds(me, 1)]

    @pl.loop(1, NDP)
    def _(o):
        req_arrival(o).wait_recv()

    to_smem = pltpu.make_async_copy(reqv, reqs, local_sem.at[1])
    to_smem.start()
    to_smem.wait()

    lane8 = lax.broadcasted_iota(jnp.int32, (8, 128), 1)

    def gather(d, lat_dst, rope_dst):
        ids = [reqs[d, 0, s] for s in range(CAP)]
        for s in range(CAP):
            lat_dst[CAP * d + s] = pool_ref[ids[s]]
        ropes = [rope_ref[ids[s]] for s in range(CAP)]
        rows = [
            jnp.where(lane8 < 64, ropes[0], ropes[1]),
            jnp.where(lane8 < 64, ropes[2], ropes[3]),
            ropes[4],
            jnp.zeros((8, 128), F32),
        ]
        rope_dst[d] = jnp.concatenate(rows, axis=0).astype(BF16)

    def lat_copy(p):
        part = pl.ds(CAP * p, CAP)
        mine = pl.ds(CAP * me, CAP)
        return remote(slat.at[part], rlat.at[mine], lat_ss.at[p], lat_rs.at[me], (p, h))

    def lat_arrival(p):
        part = pl.ds(CAP * p, CAP)
        return remote(slat.at[part], rlat.at[part], lat_ss.at[p], lat_rs.at[p], (p, h))

    def rope_copy(p):
        return remote(srope.at[p], rrope.at[me], rope_ss.at[p], rope_rs.at[me], (p, h))

    def rope_arrival(p):
        return remote(srope.at[p], rrope.at[p], rope_ss.at[p], rope_rs.at[p], (p, h))

    @pl.loop(1, NDP)
    def _(o):
        p = dp_peer(o)
        gather(p, slat, srope)
        lat_copy(p).start()
        rope_copy(p).start()

    gather(me, rlat, rrope)

    def qr_copy(k):
        p = head_peer(k)
        rows = pl.ds(h * 64, 64)
        return remote(qr_ref.at[p], qrm.at[rows], qr_ss.at[k], qr_rs.at[k], (me, p))

    def qr_arrival(k):
        p = (h + NH - k) % NH
        rows = pl.ds(p * 64, 64)
        return remote(qr_ref.at[p], qrm.at[rows], qr_ss.at[k], qr_rs.at[k], (me, p))

    for k in range(1, NH):
        qr_copy(k).start()
    qr_own = pltpu.make_async_copy(qr_ref.at[h], qrm.at[pl.ds(h * 64, 64)], local_sem.at[2])
    qr_own.start()

    x_stage(wk_ref, wkf, wk_ss, wk_rs, local_sem.at[0])
    z_stage(wv_ref, wvf, wv_ss, wv_rs, local_sem.at[3])
    core_stage(wkf, wk_ss, wk_rs)
    core_arrival(wkf, wk_ss, wk_rs).wait_recv()

    sub8 = lax.broadcasted_iota(jnp.int32, (4, 8, LAT), 1)
    for quad in range(4):
        even, odd = [], []
        for pair in range(2):
            tiles = []
            for one in range(2):
                g = quad * 4 + pair * 2 + one
                weight = wkf[:, :, :, g].reshape(LAT, NOPE)
                tiles.append(dot_nt(qn_ref[:, g * NOPE : (g + 1) * NOPE], weight).reshape(4, 8, LAT))
            a, b = tiles
            even.append(jnp.where(sub8 < 4, a, pltpu.roll(b, 4, 1)))
            odd.append(jnp.where(sub8 < 4, pltpu.roll(a, 4, 1), b))
        rows = pl.ds(quad * 16, 16)
        qsend[:, 0, rows, :] = jnp.concatenate(even, axis=1).astype(BF16)
        qsend[:, 1, rows, :] = jnp.concatenate(odd, axis=1).astype(BF16)

    def q_copy(k):
        p = head_peer(k)
        rows = pl.ds(h * 64, 64)
        return remote(qsend.at[p // 2, p % 2], qmat.at[rows], q_ss.at[k], q_rs.at[k], (me, p))

    def q_arrival(k):
        p = (h + NH - k) % NH
        rows = pl.ds(p * 64, 64)
        return remote(qsend.at[p // 2, p % 2], qmat.at[rows], q_ss.at[k], q_rs.at[k], (me, p))

    for k in range(1, NH):
        q_copy(k).start()
    q_own = pltpu.make_async_copy(
        qsend.at[h // 2, h % 2], qmat.at[pl.ds(h * 64, 64)], local_sem.at[4]
    )
    q_own.start()

    x_stage(wv_ref, wvf, wv_ss, wv_rs, local_sem.at[3])
    core_stage(wvf, wv_ss, wv_rs)

    @pl.loop(1, NDP)
    def _(o):
        p = dp_peer(o)
        lat_arrival(p).wait_recv()
        rope_arrival(p).wait_recv()

    @pl.loop(0, NDP)
    def _(d):
        rropef[pl.ds(4 * d, 4)] = rrope[d].astype(F32).reshape(4, 8, 128)

    def c_copy(r, k):
        rows = pl.ds(h * 64, 64)
        return remote(clat.at[r], kmat.at[:, rows], c_ss.at[k], c_rs.at[k], (me, r))

    def c_arrival(k):
        p = (h + NH - k) % NH
        rows = pl.ds(p * 64, 64)
        return remote(clat.at[p], kmat.at[:, rows], c_ss.at[k], c_rs.at[k], (me, p))

    def cr_copy(r, k):
        rows = pl.ds(h * 64, 64)
        return remote(crope.at[r], kr.at[rows], cr_ss.at[k], cr_rs.at[k], (me, r))

    def cr_arrival(k):
        p = (h + NH - k) % NH
        rows = pl.ds(p * 64, 64)
        return remote(crope.at[p], kr.at[rows], cr_ss.at[k], cr_rs.at[k], (me, p))

    def side(entry, want):
        code = rtab_ref[entry]
        value = rropef[code // 2]
        turn = jnp.full((8, 128), code % 2, jnp.int32) != want
        return jnp.where(turn, pltpu.roll(value, 64, 1), value)

    def compact(r):
        for quarter in range(4):
            rows = pl.ds(quarter * 16, 16)
            for b in range(2):
                entry = r * 16 + b * 8 + quarter * 2
                first = rlat[slot_ref[entry]].astype(F32)
                second = rlat[slot_ref[entry + 1]].astype(F32)
                for j in range(4):
                    tile = jnp.concatenate(
                        [first[8 * j : 8 * j + 8], second[8 * j : 8 * j + 8]], axis=0
                    )
                    clat[r, b, rows, 128 * j : 128 * j + 128] = tile.astype(BF16)
            ropes = []
            for one in range(2):
                entry = r * 16 + quarter * 2 + one
                ropes.append(jnp.where(lane8 < 64, side(entry, 0), side(entry + 8, 1)))
            crope[r, rows, :] = jnp.concatenate(ropes, axis=0).astype(BF16)

    @pl.loop(1, NH)
    def _(k):
        r = head_peer(k)
        compact(r)
        c_copy(r, k).start()
        cr_copy(r, k).start()

    compact(h)
    own_rows = pl.ds(h * 64, 64)
    c_own = pltpu.make_async_copy(clat.at[h], kmat.at[:, own_rows], local_sem.at[5])
    cr_own = pltpu.make_async_copy(crope.at[h], kr.at[own_rows], local_sem.at[6])
    c_own.start()
    cr_own.start()

    qr_own.wait()
    q_own.wait()
    for k in range(1, NH):
        qr_arrival(k).wait_recv()
        q_arrival(k).wait_recv()
    c_own.wait()
    cr_own.wait()
    for k in range(1, NH):
        c_arrival(k).wait_recv()
        cr_arrival(k).wait_recv()

    length = len_ref[h]
    newl = jnp.concatenate([newl_ref[h], jnp.zeros((112, LAT), BF16)], axis=0)
    newr = jnp.concatenate([newr_ref[h], jnp.zeros((112, 128), BF16)], axis=0)
    column = lax.broadcasted_iota(jnp.int32, (1, 512), 1)
    token0 = ((column // 8) % 8) * 64 + (column // 64) * 8 + column % 8
    neg = -jnp.inf

    def o_copy(p, k):
        return remote(osend.at[pl.ds(p * 64, 64)], oall.at[h], o_ss.at[k], o_rs.at[k], (me, p))

    def o_arrival(k):
        p = (h + NH - k) % NH
        return remote(osend.at[pl.ds(p * 64, 64)], oall.at[p], o_ss.at[k], o_rs.at[k], (me, p))

    def attend(block):
        rows = pl.ds(pl.multiple_of(block * 128, 128), 128)
        q = qmat[rows, :]
        qrot = qrm[rows, :]
        turned = pltpu.roll(qrot.astype(F32), 64, 1).astype(BF16)
        s0 = (dot_nt(q, kmat[0]) + dot_nt(qrot, kr[...])) * SCALE
        s1 = (dot_nt(q, kmat[1]) + dot_nt(turned, kr[...])) * SCALE
        s2 = (dot_nt(q, newl) + dot_nt(qrot, newr)) * SCALE
        s0 = jnp.where(token0 < length, s0, neg)
        s1 = jnp.where(token0 + 512 < length, s1, neg)
        step = lax.broadcasted_iota(jnp.int32, (128, 128), 0) % 4
        s2 = jnp.where(lax.broadcasted_iota(jnp.int32, (128, 128), 1) <= step, s2, neg)
        top = jnp.maximum(
            jnp.maximum(jnp.max(s0, axis=1, keepdims=True), jnp.max(s1, axis=1, keepdims=True)),
            jnp.max(s2, axis=1, keepdims=True),
        )
        e0, e1, e2 = jnp.exp(s0 - top), jnp.exp(s1 - top), jnp.exp(s2 - top)
        total = (
            jnp.sum(e0, axis=1, keepdims=True)
            + jnp.sum(e1, axis=1, keepdims=True)
            + jnp.sum(e2, axis=1, keepdims=True)
        )
        inv = 1.0 / total
        o = dot_nn((e0 * inv).astype(BF16), kmat[0])
        o = o + dot_nn((e1 * inv).astype(BF16), kmat[1])
        o = o + dot_nn((e2 * inv).astype(BF16), newl)
        osend[rows, :] = o.astype(BF16)

    @pl.loop(1, 4)
    def _(i):
        block = (h // 2 + i) % 4
        attend(block)
        for one in range(2):
            p = 2 * block + one
            o_copy(p, (p + NH - h) % NH).start()

    attend(h // 2)
    partner = 2 * (h // 2) + 1 - h % 2
    o_copy(partner, (partner + NH - h) % NH).start()
    oall[pl.ds(h, 1)] = osend[pl.ds(pl.multiple_of(h * 64, 64), 64), :].reshape(1, 64, LAT)

    core_arrival(wvf, wv_ss, wv_rs).wait_recv()
    for k in range(1, NH):
        o_arrival(k).wait_recv()

    for quad in range(4):
        rows = pl.ds(quad * 16, 16)
        o_rows = oall[:, rows, :].astype(F32).reshape(4, 2, 16, LAT)
        for pair in range(2):
            even = o_rows[:, 0, pair * 8 : pair * 8 + 8]
            odd = o_rows[:, 1, pair * 8 : pair * 8 + 8]
            a = jnp.where(sub8 < 4, even, pltpu.roll(odd, 4, 1))
            b = jnp.where(sub8 < 4, pltpu.roll(even, 4, 1), odd)
            for one, value in enumerate((a, b)):
                g = quad * 4 + pair * 2 + one
                weight = wvf[:, :, :, g].reshape(LAT, DV)
                result = dot_nn(value.reshape(32, LAT).astype(BF16), weight)
                out_ref[:, g * DV : (g + 1) * DV] = result.astype(BF16)

    @pl.loop(1, NDP)
    def _(o):
        p = dp_peer(o)
        req_copy(o).wait_send()
        lat_copy(p).wait_send()
        rope_copy(p).wait_send()

    weights_sent(wk_ref, wkf, wk_ss, wk_rs)
    weights_sent(wv_ref, wvf, wv_ss, wv_rs)
    for k in range(1, NH):
        qr_copy(k).wait_send()
        q_copy(k).wait_send()
        c_copy(head_peer(k), k).wait_send()
        cr_copy(head_peer(k), k).wait_send()
        o_copy(head_peer(k), k).wait_send()


def per_device(
    q_nope,
    q_rope,
    new_latent,
    new_rope,
    pool_latent,
    pool_rope,
    kv_weight,
    src_dev,
    src_block,
    lengths,
):
    entries = src_block.shape[0]
    dev = src_dev[:, 0]
    ids = jnp.arange(entries, dtype=jnp.int32)
    same = (dev[:, None] == dev[None, :]) & (ids[:, None] < ids[None, :])
    rank = jnp.sum(same.astype(jnp.int32), axis=0)
    slots = dev * CAP + rank
    rtab = dev * 8 + rank
    lanes = jnp.arange(128, dtype=jnp.int32)
    code = jnp.arange(NDP, dtype=jnp.int32)[:, None] * 128 + lanes[None, :]
    hit = code[:, :, None] == (dev * 128 + rank)[None, None, :]
    req = jnp.sum(jnp.where(hit, src_block[None, None, :], 0), axis=2).reshape(NDP, 1, 128)

    blocks = pool_latent.shape[0]
    pool = pool_latent.reshape(blocks, 8, 4, 128).transpose(0, 2, 1, 3).reshape(blocks, 32, 128)
    rope = pool_rope.reshape(blocks, 8, ROPE).astype(F32)
    rope = jnp.concatenate([rope, rope], axis=-1)
    weight = kv_weight.transpose(1, 0, 2)
    wk, wv = weight[:, :, :NOPE], weight[:, :, NOPE:]

    requests, steps = q_nope.shape[0], q_nope.shape[1]
    positions = (lengths[:, None] + jnp.arange(steps, dtype=jnp.int32)[None, :]).astype(F32)
    q_rot = rotate(
        q_rope.reshape(requests, steps, 16, ROPE).astype(F32), positions[:, :, None]
    ).astype(BF16)
    q_rot = q_rot.transpose(0, 2, 1, 3).reshape(requests, 64, ROPE)
    q_rot = jnp.pad(q_rot, ((0, 0), (0, 0), (0, 128 - ROPE)))
    k_new = rotate(new_rope.astype(F32), positions).astype(BF16)
    k_new = jnp.pad(k_new, ((0, 0), (0, 16 - steps), (0, 128 - ROPE)))
    new_lat = jnp.pad(new_latent, ((0, 0), (0, 16 - steps), (0, 0)))
    qn = q_nope.reshape(requests * steps, 16 * NOPE)

    vm = pl.BlockSpec(memory_space=pltpu.VMEM)
    sm = pl.BlockSpec(memory_space=pltpu.SMEM)
    dma = pltpu.SemaphoreType.DMA
    out = pl.pallas_call(
        kernel,
        out_shape=jax.ShapeDtypeStruct((requests * steps, 16 * DV), BF16),
        in_specs=[vm, sm, sm, sm, vm, vm, vm, vm, vm, vm, vm, vm],
        out_specs=vm,
        scratch_shapes=[
            pltpu.VMEM((NDP, 1, 128), jnp.int32),
            pltpu.SMEM((NDP, 1, 128), jnp.int32),
            pltpu.VMEM((NDP * CAP, 32, 128), BF16),
            pltpu.VMEM((NDP, 32, 128), BF16),
            pltpu.VMEM((NDP * CAP, 32, 128), BF16),
            pltpu.VMEM((NDP, 32, 128), BF16),
            pltpu.VMEM((NDP * 4, 8, 128), F32),
            pltpu.VMEM((NH, 2, 64, LAT), BF16),
            pltpu.VMEM((NH, 64, 128), BF16),
            pltpu.VMEM((2, 512, LAT), BF16),
            pltpu.VMEM((512, 128), BF16),
            pltpu.VMEM((4, 4, 2, 16, 16, 128), BF16),
            pltpu.VMEM((4, 4, 2, 16, 16, 128), BF16),
            pltpu.VMEM((4, 2, 64, LAT), BF16),
            pltpu.VMEM((512, LAT), BF16),
            pltpu.VMEM((512, 128), BF16),
            pltpu.VMEM((512, LAT), BF16),
            pltpu.VMEM((NH, 64, LAT), BF16),
            dma((7,)),
            dma((NDP,)), dma((NDP,)), dma((NDP,)), dma((NDP,)), dma((NDP,)), dma((NDP,)),
            dma((8,)), dma((8,)), dma((8,)), dma((8,)),
            dma((NH,)), dma((NH,)), dma((NH,)), dma((NH,)), dma((NH,)), dma((NH,)),
            dma((NH,)), dma((NH,)), dma((NH,)), dma((NH,)),
        ],
        compiler_params=pltpu.CompilerParams(
            collective_id=0, has_side_effects=True, vmem_limit_bytes=48 << 20
        ),
    )(req, slots, rtab, lengths, pool, rope, wk, wv, qn, q_rot, new_lat, k_new)
    return out.reshape(requests, steps, 16 * DV)


def solution(mesh):
    in_specs = (
        P("dp", None, "head"),
        P("dp", None, "head"),
        P("dp", None, None),
        P("dp", None, None),
        P("dp", "head", None),
        P("dp", "head"),
        P("dp", "head", None),
        P("dp", None),
        P("dp"),
        P("dp"),
    )
    out_specs = P("dp", None, "head")
    return jax.shard_map(
        per_device, mesh=mesh, in_specs=in_specs, out_specs=out_specs, check_vma=False
    )
```

time: 598 us -> 114 us (0.19); the launches traced: 587 us -> 114 us
  waiting for transfers between devices: 345 us -> 0 us
  blocking collectives: 175 us -> 0 us
  Pallas kernels: 0 us -> 107 us
  local copies, waits for them, and re-layouts: 26.6 us -> 3.17 us
  between operations: 15.2 us -> 0.19 us
  matrix products: 12.1 us -> 0 us
  starting transfers between devices: 10.1 us -> 0 us
    all_gather x3 -> x0, waiting for transfers between devices: 345 us -> none  [the longest x1 238 us: per_device(): weights = lax.all_gather(kv_weight, 'dp', axis=0, tiled=True)]
    pallas_call x0 -> x1, Pallas kernels: none -> 107 us  [per_device(): pl.pallas_call(kernel, out_shape=jax.ShapeDtypeStruct((requests * steps,...]
    all_gather x2 -> x0, blocking collectives: 87.7 us -> none  [the longest x1 48.7 us: per_device(): lax.all_gather(src_dev, 'dp', axis=0, tiled=True)]
    all_to_all x1 -> x0, blocking collectives: 86.9 us -> none  [per_device(): lax.all_to_all(full_rope, 'dp', split_axis=0, concat_axis=0, tiled=True)]
    gather x5 -> x0, local copies, waits for them, and re-layouts: 17.4 us -> none  [the longest x1 10.6 us: per_device(): recv_lat.reshape(dp_count * capacity, block_len, LAT)[slot_index]]
    dot_general x8 -> x0, matrix products: 12.1 us -> none  [the longest x1 5.99 us: per_device(): jnp.einsum('rql,rtl->rqt', queries, cache_lat, preferred_element_type=jnp...]
    all_to_all x1 -> x0, starting transfers between devices: 9.8 us -> none  [per_device(): lax.all_to_all(full_lat, 'dp', split_axis=0, concat_axis=0, tiled=True)]
  transfers between devices with their start and end apart: 4 -> 0, of which waited for: 3 -> 0; matrix products, arithmetic and copies ran while one was open for 3% -> 0% of each run, Pallas kernels for 0% -> 0%
where the time goes in v1:
time: 114 us
  Pallas kernels  107 us (94%)
  other arithmetic  3.7 us (3%)
  local copies, waits for them, and re-layouts  3.17 us (3%)
    pallas_call x1, Pallas kernels, per_device(): pl.pallas_call(kernel, out_shape=jax.ShapeDtypeStruct((requests * steps,...  107 us

profile of v1, /device:TPU:1, one launch (start us, length us, event | category | flops | bytes accessed | tf_op | source)
XLA Modules:
  0.0 113.7 jit_solution(9392144286926245355)
XLA Ops:
  0.0 0.7 convert_element_type.40
  0.7 0.7 add_convert_fusion.2
  1.4 0.2 subtract_convert_fusion.1
  1.6 1.0 reshape.131
  2.6 0.1 fusion.7
  2.8 0.2 subtract_convert_fusion
  3.0 0.0 copy-start.7
  3.0 0.0 copy-start.6
  3.0 0.0 copy-start.2
  3.0 0.2 pad_maximum_fusion
  3.3 0.1 fusion.6.newr_ref
  3.4 0.3 copy-done.7
  3.7 0.1 convert_reduce_fusion
  3.8 0.1 iota_add_fusion
  3.9 1.3 %select_reduce_fusion = s32[32,128]{1,0:T(8,128)S(1)} fusion(s32[128]{0:T(128)S(1)} %copy-done.6, s32[128]{0:T(128)S(1)} %get-tuple-element.17, s32[32,128]{1,0:T(8,128)S(1)} %iota_add_fusion), kind=kLoop, calls=%fused_computation | loop fusion | flops 1568768 | bytes 33792 | tf_op jit(solution)/shard_map/reduce_sum | solution.py:440
  5.2 0.0 copy-start.3
  5.3 0.0 copy-start.1
  5.3 0.1 convert_element_type.36
  5.4 0.1 maximum_convert_fusion.rope_ref
  5.5 0.4 copy-done.5
  5.9 0.2 copy-done.3
  6.2 0.2 copy-done
  6.3 106.7 %shard_map.100 = bf16[32,2048]{1,0:T(8,128)(2,1)S(1)} custom-call(s32[32,1,128]{2,1,0:T(1,128)S(1)} %bitcast.17, s32[128]{0:T(128)S(1)} %get-tuple-element.16.slot_ref, s32[128]{0:T(128)S(1)} %get-tuple-element.15.rtab_ref, s32[8]{0:T(128)S(1)} %copy-done.1, bf16[64,32,128]{2,1,0:T(8,128)(2,1)S(1)} %bitcast.16, ...), custom_call_target="tpu_custom_call" | custom-call | tf_op jit(solution)/shard_map/pallas_call | solution.py:464
  113.0 0.7 reshape.130
  (15 shorter events, 0.2 us)
Async XLA Ops:
  3.0 0.7 copy-start.7
  3.0 0.8 copy-start.6
  3.0 2.1 %copy-start.2 = (bf16[16,16,256]{2,1,0:T(8,128)(2,1)S(1)}, bf16[16,16,256]{2,1,0:T(8,128)(2,1)}, u32[]{:S(2)}) copy-start(bf16[16,16,256]{2,1,0:T(8,128)(2,1)} %param.16) | copy-start | bytes 393220
  3.2 2.1 %copy-start.4 = (bf16[64,512]{1,0:T(8,128)(2,1)S(1)}, bf16[64,512]{1,0:T(8,128)(2,1)}, u32[]{:S(2)}) copy-start(bf16[64,512]{1,0:T(8,128)(2,1)} %param.15) | copy-start | bytes 196612
  5.1 0.8 copy-start.5
  5.2 0.9 copy-start.3
  5.3 1.1 copy-start
  5.3 1.1 copy-start.1

commit v2 on v1

v2 whole, which is shorter than its diff:
```python
import jax
import jax.numpy as jnp
import numpy as np
from jax import lax
from jax.experimental import pallas as pl
from jax.experimental.pallas import tpu as pltpu
from jax.sharding import PartitionSpec as P

LAT = 512
ROPE = 64
NOPE = 128
DV = 128
CAP = 5
NDP = 32
NH = 8
MESH = pl.DeviceIdType.MESH
F32 = jnp.float32
BF16 = jnp.bfloat16
SCALE = (NOPE + ROPE) ** (-0.5)
OTHERS = (0, 1, 2, 3, 5, 6, 7)


FREQS = np.tile(10000.0 ** (-(2.0 * np.arange(32)) / 64.0), 4).astype(np.float32).reshape(1, 128)


def rotated(values, cosine, sine):
    lane = lax.broadcasted_iota(jnp.int32, values.shape, 1) % 64
    ahead = pltpu.roll(values, 96, 1)
    behind = pltpu.roll(values, 32, 1)
    return values * cosine + jnp.where(lane < 32, -ahead, behind) * sine


def remote(src, dst, send_sem, recv_sem, device):
    return pltpu.make_async_remote_copy(
        src_ref=src,
        dst_ref=dst,
        send_sem=send_sem,
        recv_sem=recv_sem,
        device_id=device,
        device_id_type=MESH,
    )


def dot_nt(a, b):
    return lax.dot_general(a, b, (((1,), (1,)), ((), ())), preferred_element_type=F32)


def dot_nn(a, b):
    return lax.dot_general(a, b, (((1,), (0,)), ((), ())), preferred_element_type=F32)


def kernel(
    dev_ref, block_ref, len_ref, freq_ref, pool_hbm, rope_hbm, kv_hbm, qn_hbm, qr_hbm,
    newl_ref, newr_ref, out_ref,
    pool_ref, rope_ref, kv_ref, kvf, wk_ref, wv_ref, qn_ref, qr_ref, fetch_sem,
    req, tab, tabs, reqv, reqs, slat, srope, rlat, rrope, rropef, clat, crope, kmat, kr, wkf, wvf,
    qsend, qmat, osend, oall,
    local_sem, req_ss, req_rs, lat_ss, lat_rs, rope_ss, rope_rs,
    wk_ss, wk_rs, wv_ss, wv_rs, q_ss, q_rs, c_ss, c_rs, cr_ss, cr_rs, o_ss, o_rs,
):
    me = lax.axis_index("dp")
    h = lax.axis_index("head")
    x, zh, c = me // 8, (me // 2) % 4, me % 2

    def dp_peer(o):
        return ((x + o // 8) % 4) * 8 + ((zh + (o // 2) % 4) % 4) * 2 + (c + o % 2) % 2

    zl, y = h // 4, h % 4
    flip = (1 - zl) * 4 + y

    def across(o):
        return jnp.where((o // 2) % 4 == 2, flip, h)

    def head_peer(k):
        return ((zl + 1 + k // 4) % 2) * 4 + (y + k) % 4

    def head_from(k):
        return ((zl + 1 + k // 4) % 2) * 4 + (y + 4 - k % 4) % 4

    fetches = []
    for source, target in (
        (kv_hbm, kv_ref), (qr_hbm, qr_ref), (pool_hbm, pool_ref), (rope_hbm, rope_ref), (qn_hbm, qn_ref)
    ):
        fetches.append(pltpu.make_async_copy(source, target, fetch_sem.at[len(fetches)]))

    barrier = pltpu.get_barrier_semaphore()

    @pl.loop(1, NDP)
    def _(o):
        pl.semaphore_signal(
            barrier, inc=1, device_id=(dp_peer(o), across(o)), device_id_type=MESH
        )

    for k in OTHERS:
        pl.semaphore_signal(barrier, inc=1, device_id=(me, head_peer(k)), device_id_type=MESH)

    for fetch in fetches:
        fetch.start()

    dev = dev_ref[...]
    blk = block_ref[...]
    row = lax.broadcasted_iota(jnp.int32, (128, 128), 0)
    col = lax.broadcasted_iota(jnp.int32, (128, 128), 1)
    dev_rows = jnp.broadcast_to(dev, (128, 128))
    dev_col = jnp.sum(jnp.where(row == col, dev_rows, 0), axis=1, keepdims=True)
    same = jnp.where((dev_col == dev_rows) & (row < col), 1, 0)
    rank = jnp.sum(same, axis=0, keepdims=True)
    source = lax.broadcasted_iota(jnp.int32, (NDP, 128), 0)
    lanes = lax.broadcasted_iota(jnp.int32, (NDP, 128), 1)
    asked = jnp.zeros((NDP, 128), jnp.int32)
    for slot in range(CAP):
        hit = (source == dev) & (rank == slot)
        found = jnp.sum(jnp.where(hit, blk, 0), axis=1, keepdims=True)
        asked = jnp.where(lanes == slot, found, asked)
    req[...] = asked.reshape(NDP, 1, 128)
    tab[0:1, :] = dev * CAP + rank
    tab[1:2, :] = dev * 8 + rank
    tab_copy = pltpu.make_async_copy(tab, tabs, local_sem.at[2])
    tab_copy.start()

    fetches[0].wait()
    kvf[...] = kv_ref[...].astype(F32)
    for g in range(16):
        one_head = kvf[:, g, :]
        wk_ref[g] = one_head[:, :NOPE].astype(BF16)
        wv_ref[g] = one_head[:, NOPE:].astype(BF16)

    fetches[1].wait()
    low = lax.broadcasted_iota(jnp.int32, (32, 128), 1) < 64
    request = lax.broadcasted_iota(jnp.int32, (32, 128), 0)
    position = request % 4
    for r in range(8):
        position = position + jnp.where(request // 4 == r, len_ref[r], 0)
    angle = position.astype(F32) * freq_ref[...]
    cosine, sine = jnp.cos(angle), jnp.sin(angle)

    def by_request(tiles):
        width = tiles[0].shape[-1]
        first = lax.broadcasted_iota(jnp.int32, (4, 8, width), 1) < 4
        even, odd = [], []
        for pair in range(2):
            a = tiles[2 * pair].reshape(4, 8, width)
            b = tiles[2 * pair + 1].reshape(4, 8, width)
            even.append(jnp.where(first, a, pltpu.roll(b, 4, 1)))
            odd.append(jnp.where(first, pltpu.roll(a, 4, 1), b))
        return (
            jnp.concatenate(even, axis=1).astype(BF16),
            jnp.concatenate(odd, axis=1).astype(BF16),
        )

    for quad in range(4):
        tiles = []
        for pair in range(2):
            at = (quad * 2 + pair) * 128
            turned = rotated(qr_ref[:, at : at + 128].astype(F32), cosine, sine)
            tiles.append(jnp.where(low, turned, 0.0))
            tiles.append(jnp.where(low, pltpu.roll(turned, 64, 1), 0.0))
        even, odd = by_request(tiles)
        qsend[:, 0, quad * 16 : quad * 16 + 16, LAT:] = even
        qsend[:, 1, quad * 16 : quad * 16 + 16, LAT:] = odd

    pl.semaphore_wait(barrier, NDP - 1 + NH - 1)

    def req_copy(o):
        p = dp_peer(o)
        return remote(req.at[p], reqv.at[me], req_ss.at[p], req_rs.at[me], (p, across(o)))

    def req_arrival(o):
        p = dp_peer(o)
        return remote(req.at[p], reqv.at[p], req_ss.at[p], req_rs.at[p], (p, across(o)))

    def z_dev(k):
        return (x * 8 + ((zh + k) % 4) * 2 + c, h)

    def z_copy(own, full, ss, rs, k):
        return remote(own, full.at[x, zh, c], ss.at[k], rs.at[k], z_dev(k))

    def z_arrival(own, full, ss, rs, k):
        return remote(own, full.at[x, (zh + 4 - k) % 4, c], ss.at[k], rs.at[k], z_dev(k))

    def z_relay(full, ss, rs, k):
        part = full.at[x, (zh + 4 - k) % 4, c, pl.ds(0 if k == 1 else 8, 8)]
        return remote(part, part, ss.at[8 + k], rs.at[8 + k], z_dev(k))

    def z_relay_arrival(full, ss, rs, k):
        part = full.at[x, (zh + 2) % 4, c, pl.ds(0 if k == 1 else 8, 8)]
        return remote(part, part, ss.at[8 + k], rs.at[8 + k], z_dev(k))

    def x_copy(full, ss, rs, k):
        p = (((x + k) % 4) * 8 + zh * 2 + c, h)
        return remote(full.at[x, :, c], full.at[x, :, c], ss.at[3 + k], rs.at[3 + k], p)

    def x_arrival(full, ss, rs, k):
        xx = (x + 4 - k) % 4
        return remote(
            full.at[xx, :, c], full.at[xx, :, c], ss.at[3 + k], rs.at[3 + k], (xx * 8 + zh * 2 + c, h)
        )

    def core_copy(full, ss, rs):
        p = (x * 8 + zh * 2 + (1 - c), h)
        return remote(full.at[:, :, c], full.at[:, :, c], ss.at[7], rs.at[7], p)

    def core_arrival(full, ss, rs):
        p = (x * 8 + zh * 2 + (1 - c), h)
        return remote(full.at[:, :, 1 - c], full.at[:, :, 1 - c], ss.at[7], rs.at[7], p)

    def z_stage(own, full, ss, rs, sem):
        pltpu.make_async_copy(own, full.at[x, zh, c], sem).start()
        for k in (1, 3):
            z_copy(own, full, ss, rs, k).start()

    def z_pass(own, full, ss, rs):
        for k in (1, 3):
            z_arrival(own, full, ss, rs, k).wait_recv()
            z_relay(full, ss, rs, k).start()

    def x_stage(own, full, ss, rs, sem):
        pltpu.make_async_copy(own, full.at[x, zh, c], sem).wait()
        for k in (1, 3):
            z_relay_arrival(full, ss, rs, k).wait_recv()
        for k in (1, 2, 3):
            x_copy(full, ss, rs, k).start()

    def core_stage(full, ss, rs):
        for k in (1, 2, 3):
            x_arrival(full, ss, rs, k).wait_recv()
        core_copy(full, ss, rs).start()

    def weights_sent(own, full, ss, rs):
        for k in (1, 3):
            z_copy(own, full, ss, rs, k).wait_send()
            z_relay(full, ss, rs, k).wait_send()
        for k in (1, 2, 3):
            x_copy(full, ss, rs, k).wait_send()
        core_copy(full, ss, rs).wait_send()

    @pl.loop(1, NDP)
    def _(o):
        req_copy(o).start()

    z_stage(wk_ref, wkf, wk_ss, wk_rs, local_sem.at[0])
    z_stage(wv_ref, wvf, wv_ss, wv_rs, local_sem.at[3])
    reqv[pl.ds(me, 1)] = req[pl.ds(me, 1)]
    z_pass(wk_ref, wkf, wk_ss, wk_rs)
    z_pass(wv_ref, wvf, wv_ss, wv_rs)

    @pl.loop(1, NDP)
    def _(o):
        req_arrival(o).wait_recv()

    to_smem = pltpu.make_async_copy(reqv, reqs, local_sem.at[1])
    to_smem.start()
    to_smem.wait()
    x_stage(wk_ref, wkf, wk_ss, wk_rs, local_sem.at[0])
    fetches[2].wait()
    fetches[3].wait()

    lane8 = lax.broadcasted_iota(jnp.int32, (8, 128), 1)

    def gather(d, lat_dst, rope_dst):
        ids = [reqs[d, 0, s] for s in range(CAP)]
        for s in range(CAP):
            lat_dst[CAP * d + s] = pool_ref[ids[s]]
        ropes = [rope_ref[ids[s]] for s in range(CAP)]
        rows = [
            jnp.where(lane8 < 64, ropes[0], ropes[1]),
            jnp.where(lane8 < 64, ropes[2], ropes[3]),
            ropes[4],
            jnp.zeros((8, 128), F32),
        ]
        rope_dst[d] = jnp.concatenate(rows, axis=0).astype(BF16)

    def lat_copy(o):
        p = dp_peer(o)
        part = pl.ds(CAP * p, CAP)
        mine = pl.ds(CAP * me, CAP)
        return remote(slat.at[part], rlat.at[mine], lat_ss.at[p], lat_rs.at[me], (p, across(o)))

    def lat_arrival(o):
        p = dp_peer(o)
        part = pl.ds(CAP * p, CAP)
        return remote(slat.at[part], rlat.at[part], lat_ss.at[p], lat_rs.at[p], (p, across(o)))

    def rope_copy(o):
        p = dp_peer(o)
        return remote(srope.at[p], rrope.at[me], rope_ss.at[p], rope_rs.at[me], (p, across(o)))

    def rope_arrival(o):
        p = dp_peer(o)
        return remote(srope.at[p], rrope.at[p], rope_ss.at[p], rope_rs.at[p], (p, across(o)))

    @pl.loop(1, NDP)
    def _(o):
        gather(dp_peer(o), slat, srope)
        lat_copy(o).start()
        rope_copy(o).start()

    gather(me, rlat, rrope)

    core_stage(wkf, wk_ss, wk_rs)
    core_arrival(wkf, wk_ss, wk_rs).wait_recv()

    fetches[4].wait()

    for quad in range(4):
        tiles = []
        for g in range(quad * 4, quad * 4 + 4):
            weight = wkf[:, :, :, g].reshape(LAT, NOPE)
            tiles.append(dot_nt(qn_ref[:, g * NOPE : (g + 1) * NOPE], weight))
        even, odd = by_request(tiles)
        qsend[:, 0, quad * 16 : quad * 16 + 16, :LAT] = even
        qsend[:, 1, quad * 16 : quad * 16 + 16, :LAT] = odd

    def q_copy(k):
        p = head_peer(k)
        rows = pl.ds(h * 64, 64)
        return remote(qsend.at[p // 2, p % 2], qmat.at[rows], q_ss.at[k], q_rs.at[k], (me, p))

    def q_arrival(k):
        p = head_from(k)
        rows = pl.ds(p * 64, 64)
        return remote(qsend.at[p // 2, p % 2], qmat.at[rows], q_ss.at[k], q_rs.at[k], (me, p))

    for k in OTHERS:
        q_copy(k).start()
    q_own = pltpu.make_async_copy(
        qsend.at[h // 2, h % 2], qmat.at[pl.ds(h * 64, 64)], local_sem.at[4]
    )
    q_own.start()

    x_stage(wv_ref, wvf, wv_ss, wv_rs, local_sem.at[3])
    tab_copy.wait()

    @pl.loop(1, NDP)
    def _(o):
        lat_arrival(o).wait_recv()
        rope_arrival(o).wait_recv()

    @pl.loop(0, NDP)
    def _(d):
        rropef[pl.ds(4 * d, 4)] = rrope[d].astype(F32).reshape(4, 8, 128)

    def c_copy(r, k):
        rows = pl.ds(h * 64, 64)
        return remote(clat.at[r], kmat.at[:, rows], c_ss.at[k], c_rs.at[k], (me, r))

    def c_arrival(k):
        p = head_from(k)
        rows = pl.ds(p * 64, 64)
        return remote(clat.at[p], kmat.at[:, rows], c_ss.at[k], c_rs.at[k], (me, p))

    def cr_copy(r, k):
        rows = pl.ds(h * 64, 64)
        return remote(crope.at[r], kr.at[rows], cr_ss.at[k], cr_rs.at[k], (me, r))

    def cr_arrival(k):
        p = head_from(k)
        rows = pl.ds(p * 64, 64)
        return remote(crope.at[p], kr.at[rows], cr_ss.at[k], cr_rs.at[k], (me, p))

    def side(entry, want):
        code = tabs[1, entry]
        value = rropef[code // 2]
        turn = jnp.full((8, 128), code % 2, jnp.int32) != want
        return jnp.where(turn, pltpu.roll(value, 64, 1), value)

    def compact(r):
        for quarter in range(4):
            rows = pl.ds(quarter * 16, 16)
            for b in range(2):
                entry = r * 16 + b * 8 + quarter * 2
                first = rlat[tabs[0, entry]].astype(F32)
                second = rlat[tabs[0, entry + 1]].astype(F32)
                for j in range(4):
                    tile = jnp.concatenate(
                        [first[8 * j : 8 * j + 8], second[8 * j : 8 * j + 8]], axis=0
                    )
                    clat[r, b, rows, 128 * j : 128 * j + 128] = tile.astype(BF16)
            ropes = []
            for one in range(2):
                entry = r * 16 + quarter * 2 + one
                ropes.append(jnp.where(lane8 < 64, side(entry, 0), side(entry + 8, 1)))
            crope[r, rows, :] = jnp.concatenate(ropes, axis=0).astype(BF16)

    @pl.loop(0, NH)
    def _(k):
        @pl.when(k != 4)
        def _():
            r = head_peer(k)
            compact(r)
            c_copy(r, k).start()
            cr_copy(r, k).start()

    compact(h)
    own_rows = pl.ds(h * 64, 64)
    c_own = pltpu.make_async_copy(clat.at[h], kmat.at[:, own_rows], local_sem.at[5])
    cr_own = pltpu.make_async_copy(crope.at[h], kr.at[own_rows], local_sem.at[6])
    c_own.start()
    cr_own.start()
    core_stage(wvf, wv_ss, wv_rs)

    q_own.wait()
    for k in OTHERS:
        q_arrival(k).wait_recv()
    c_own.wait()
    cr_own.wait()
    for k in OTHERS:
        c_arrival(k).wait_recv()
        cr_arrival(k).wait_recv()

    length = len_ref[h]
    newl = jnp.concatenate([newl_ref[h], jnp.zeros((112, LAT), BF16)], axis=0)
    place = length + lax.broadcasted_iota(jnp.int32, (8, 128), 0)
    angle_new = place.astype(F32) * freq_ref[...]
    turned_new = rotated(newr_ref[h], jnp.cos(angle_new), jnp.sin(angle_new))
    newr = jnp.concatenate([turned_new, jnp.zeros((120, 128), F32)], axis=0).astype(BF16)
    column = lax.broadcasted_iota(jnp.int32, (1, 512), 1)
    of_entry = (column // 8) % 8
    tokens = []
    for b in range(2):
        moved = jnp.zeros((1, 512), jnp.int32)
        for e in range(8):
            code = tabs[1, h * 16 + b * 8 + e]
            far = (code // 16 + 4 - zh) % 4
            moved = jnp.where(of_entry == e, far, moved)
        part = jnp.where(moved == 2, (column // 64 + 4) % 8, column // 64)
        tokens.append((of_entry + 8 * b) * 64 + part * 8 + column % 8)
    neg = -jnp.inf

    def o_copy(p, k):
        return remote(osend.at[pl.ds(p * 64, 64)], oall.at[h], o_ss.at[k], o_rs.at[k], (me, p))

    def o_arrival(k):
        p = head_from(k)
        return remote(osend.at[pl.ds(p * 64, 64)], oall.at[p], o_ss.at[k], o_rs.at[k], (me, p))

    def step_to(p):
        return ((p // 4 + zl + 1) % 2) * 4 + (p + 4 - y) % 4

    def attend(block):
        rows = pl.ds(pl.multiple_of(block * 128, 128), 128)
        q = qmat[rows, :LAT]
        qrot = qmat[rows, LAT:]
        turned = pltpu.roll(qrot.astype(F32), 64, 1).astype(BF16)
        s0 = (dot_nt(q, kmat[0]) + dot_nt(qrot, kr[...])) * SCALE
        s1 = (dot_nt(q, kmat[1]) + dot_nt(turned, kr[...])) * SCALE
        s2 = (dot_nt(q, newl) + dot_nt(qrot, newr)) * SCALE
        s0 = jnp.where(tokens[0] < length, s0, neg)
        s1 = jnp.where(tokens[1] < length, s1, neg)
        step = lax.broadcasted_iota(jnp.int32, (128, 128), 0) % 4
        s2 = jnp.where(lax.broadcasted_iota(jnp.int32, (128, 128), 1) <= step, s2, neg)
        top = jnp.maximum(
            jnp.maximum(jnp.max(s0, axis=1, keepdims=True), jnp.max(s1, axis=1, keepdims=True)),
            jnp.max(s2, axis=1, keepdims=True),
        )
        e0, e1, e2 = jnp.exp(s0 - top), jnp.exp(s1 - top), jnp.exp(s2 - top)
        total = (
            jnp.sum(e0, axis=1, keepdims=True)
            + jnp.sum(e1, axis=1, keepdims=True)
            + jnp.sum(e2, axis=1, keepdims=True)
        )
        inv = 1.0 / total
        o = dot_nn((e0 * inv).astype(BF16), kmat[0])
        o = o + dot_nn((e1 * inv).astype(BF16), kmat[1])
        o = o + dot_nn((e2 * inv).astype(BF16), newl)
        osend[rows, :] = o.astype(BF16)

    @pl.loop(0, 3)
    def _(i):
        half = (zl + 1 + i // 2) % 2
        block = half * 2 + (y // 2 + (i + 1) // 2) % 2
        attend(block)
        for one in range(2):
            p = 2 * block + one
            o_copy(p, step_to(p)).start()

    attend(h // 2)
    partner = 2 * (h // 2) + 1 - h % 2
    o_copy(partner, step_to(partner)).start()
    oall[pl.ds(h, 1)] = osend[pl.ds(pl.multiple_of(h * 64, 64), 64), :].reshape(1, 64, LAT)

    core_arrival(wvf, wv_ss, wv_rs).wait_recv()
    for k in OTHERS:
        o_arrival(k).wait_recv()

    first4 = lax.broadcasted_iota(jnp.int32, (4, 8, LAT), 1) < 4
    for quad in range(4):
        rows = pl.ds(quad * 16, 16)
        o_rows = oall[:, rows, :].astype(F32).reshape(4, 2, 16, LAT)
        for pair in range(2):
            even = o_rows[:, 0, pair * 8 : pair * 8 + 8]
            odd = o_rows[:, 1, pair * 8 : pair * 8 + 8]
            a = jnp.where(first4, even, pltpu.roll(odd, 4, 1))
            b = jnp.where(first4, pltpu.roll(even, 4, 1), odd)
            for one, value in enumerate((a, b)):
                g = quad * 4 + pair * 2 + one
                weight = wvf[:, :, :, g].reshape(LAT, DV)
                result = dot_nn(value.reshape(32, LAT).astype(BF16), weight)
                out_ref[:, g * DV : (g + 1) * DV] = result.astype(BF16)

    @pl.loop(1, NDP)
    def _(o):
        req_copy(o).wait_send()
        lat_copy(o).wait_send()
        rope_copy(o).wait_send()

    weights_sent(wk_ref, wkf, wk_ss, wk_rs)
    weights_sent(wv_ref, wvf, wv_ss, wv_rs)
    for k in OTHERS:
        q_copy(k).wait_send()
        c_copy(head_peer(k), k).wait_send()
        cr_copy(head_peer(k), k).wait_send()
        o_copy(head_peer(k), k).wait_send()


def per_device(
    q_nope,
    q_rope,
    new_latent,
    new_rope,
    pool_latent,
    pool_rope,
    kv_weight,
    src_dev,
    src_block,
    lengths,
):
    blocks = pool_latent.shape[0]
    pool = pool_latent.reshape(blocks, 8, 4, 128).transpose(0, 2, 1, 3).reshape(blocks, 32, 128)
    rope = pool_rope.reshape(blocks, 8, ROPE).astype(F32)
    rope = jnp.concatenate([rope, rope], axis=-1)
    requests, steps = q_nope.shape[0], q_nope.shape[1]
    qr = q_rope.reshape(requests * steps, 16 * ROPE)
    new_rot = jnp.pad(new_rope.astype(F32), ((0, 0), (0, 8 - steps), (0, 128 - ROPE)))
    new_lat = jnp.pad(new_latent, ((0, 0), (0, 16 - steps), (0, 0)))
    qn = q_nope.reshape(requests * steps, 16 * NOPE)

    vm = pl.BlockSpec(memory_space=pltpu.VMEM)
    sm = pl.BlockSpec(memory_space=pltpu.SMEM)
    hbm = pl.BlockSpec(memory_space=pl.ANY)
    dma = pltpu.SemaphoreType.DMA
    out = pl.pallas_call(
        kernel,
        out_shape=jax.ShapeDtypeStruct((requests * steps, 16 * DV), BF16),
        in_specs=[vm, vm, sm, vm, hbm, hbm, hbm, hbm, hbm, vm, vm],
        out_specs=vm,
        scratch_shapes=[
            pltpu.VMEM((blocks, 32, 128), BF16),
            pltpu.VMEM((blocks, 8, 128), F32),
            pltpu.VMEM((16, 16, NOPE + DV), BF16),
            pltpu.VMEM((16, 16, NOPE + DV), F32),
            pltpu.VMEM((16, 16, NOPE), BF16),
            pltpu.VMEM((16, 16, DV), BF16),
            pltpu.VMEM((32, 16 * NOPE), BF16),
            pltpu.VMEM((32, 16 * ROPE), BF16),
            dma((5,)),
            pltpu.VMEM((NDP, 1, 128), jnp.int32),
            pltpu.VMEM((8, 128), jnp.int32),
            pltpu.SMEM((8, 128), jnp.int32),
            pltpu.VMEM((NDP, 1, 128), jnp.int32),
            pltpu.SMEM((NDP, 1, 128), jnp.int32),
            pltpu.VMEM((NDP * CAP, 32, 128), BF16),
            pltpu.VMEM((NDP, 32, 128), BF16),
            pltpu.VMEM((NDP * CAP, 32, 128), BF16),
            pltpu.VMEM((NDP, 32, 128), BF16),
            pltpu.VMEM((NDP * 4, 8, 128), F32),
            pltpu.VMEM((NH, 2, 64, LAT), BF16),
            pltpu.VMEM((NH, 64, 128), BF16),
            pltpu.VMEM((2, 512, LAT), BF16),
            pltpu.VMEM((512, 128), BF16),
            pltpu.VMEM((4, 4, 2, 16, 16, 128), BF16),
            pltpu.VMEM((4, 4, 2, 16, 16, 128), BF16),
            pltpu.VMEM((4, 2, 64, LAT + 128), BF16),
            pltpu.VMEM((512, LAT + 128), BF16),
            pltpu.VMEM((512, LAT), BF16),
            pltpu.VMEM((NH, 64, LAT), BF16),
            dma((7,)),
            dma((NDP,)), dma((NDP,)), dma((NDP,)), dma((NDP,)), dma((NDP,)), dma((NDP,)),
            dma((12,)), dma((12,)), dma((12,)), dma((12,)),
            dma((NH,)), dma((NH,)), dma((NH,)), dma((NH,)),
            dma((NH,)), dma((NH,)), dma((NH,)), dma((NH,)),
        ],
        compiler_params=pltpu.CompilerParams(
            collective_id=0, has_side_effects=True, vmem_limit_bytes=48 << 20
        ),
    )(
        src_dev.reshape(1, -1), src_block.reshape(1, -1), lengths, jnp.asarray(FREQS),
        pool, rope, kv_weight, qn, qr, new_lat, new_rot,
    )
    return out.reshape(requests, steps, 16 * DV)


def solution(mesh):
    in_specs = (
        P("dp", None, "head"),
        P("dp", None, "head"),
        P("dp", None, None),
        P("dp", None, None),
        P("dp", "head", None),
        P("dp", "head"),
        P("dp", "head", None),
        P("dp", None),
        P("dp"),
        P("dp"),
    )
    out_specs = P("dp", None, "head")
    return jax.shard_map(
        per_device, mesh=mesh, in_specs=in_specs, out_specs=out_specs, check_vma=False
    )
```

time: 114 us -> 96.4 us (0.85)
  Pallas kernels: 107 us -> 92.7 us
  other arithmetic: 3.7 us -> 0.84 us
    pallas_call x1, Pallas kernels: 107 us -> 92.7 us  [per_device(): pl.pallas_call(kernel, out_shape=jax.ShapeDtypeStruct((requests * steps,...]
    convert_element_type x2 -> x0, other arithmetic: 1.43 us -> none  [the longest x1 0.73 us: per_device(): (lengths[:, None] + jnp.arange(steps, dtype=jnp.int32)[None, :]).astype(F32)]
    reduce_sum x2 -> x0, other arithmetic: 1.37 us -> none  [the longest x1 1.28 us: per_device(): jnp.sum(jnp.where(hit, src_block[None, None, :], 0), axis=2)]
where the time goes in v2:
time: 96.4 us; the launch traced here: 96.2 us
  Pallas kernels  92.7 us (96%)
  local copies, waits for them, and re-layouts  2.61 us (3%)
    pallas_call x1, Pallas kernels, per_device(): pl.pallas_call(kernel, out_shape=jax.ShapeDtypeStruct((requests * steps,...  92.7 us

profile of v2, /device:TPU:1, one launch (start us, length us, event | category | flops | bytes accessed | tf_op | source)
XLA Modules:
  0.0 96.2 jit_solution(16821841736486720500)
XLA Ops:
  0.0 0.0 copy-start.6
  0.0 0.7 pad_convert_fusion.newr_ref
  0.7 0.0 copy-start.8
  0.7 0.0 copy-start.7
  0.8 0.9 reshape.29.qr_hbm
  1.6 0.0 copy-done.6
  1.7 0.0 copy-start
  1.7 0.0 copy-done.8
  1.7 0.0 copy-done.7
  1.8 0.1 convert_element_type.9
  1.9 0.0 copy-start.1
  1.9 0.0 copy-start.2
  1.9 0.0 copy-start.3
  1.9 0.0 copy-start.4
  1.9 0.0 copy-start.5
  1.9 0.1 maximum_convert_fusion.rope_hbm
  2.1 0.6 copy-done
  2.7 0.1 copy-done.1
  2.8 0.0 copy-done.2
  2.8 0.0 copy-done.3
  2.8 0.0 copy-done.4
  2.8 0.0 copy-done.5
  2.8 92.7 %shard_map.109 = bf16[32,2048]{1,0:T(8,128)(2,1)S(1)} custom-call(s32[1,128]{1,0:T(1,128)S(1)} %bitcast.8, s32[1,128]{1,0:T(1,128)S(1)} %bitcast.9, s32[8]{0:T(128)S(1)} %copy-done.4, f32[1,128]{1,0:T(1,128)S(1)} %copy-done.5, bf16[64,32,128]{2,1,0:T(8,128)(2,1)S(1)} %bitcast.7, f32[64,8,128]{2,1,0:T(8,128)S(1)} %maximum_convert_fusion.rope_hbm, ...), custom_call_target="tpu_custom_call" | custom-call | tf_op jit(solution)/shard_map/pallas_call | solution.py:542
  95.5 0.7 reshape.30
  (2 shorter events, 0.1 us)
Async XLA Ops:
  0.0 1.6 %copy-start.6 = (bf16[8,4,2048]{2,1,0:T(4,128)(2,1)S(1)}, bf16[8,4,2048]{2,1,0:T(4,128)(2,1)}, u32[]{:S(2)}) copy-start(bf16[8,4,2048]{2,1,0:T(4,128)(2,1)} %param.11) | copy-start | bytes 393220
  0.7 1.0 %copy-start.8 = (bf16[8,4,512]{2,1,0:T(4,128)(2,1)S(1)}, bf16[8,4,512]{2,1,0:T(4,128)(2,1)}, u32[]{:S(2)}) copy-start(bf16[8,4,512]{2,1,0:T(4,128)(2,1)} %param.13) | copy-start | bytes 98308
  0.7 1.0 %copy-start.7 = (bf16[64,512]{1,0:T(8,128)(2,1)S(1)}, bf16[64,512]{1,0:T(8,128)(2,1)}, u32[]{:S(2)}) copy-start(bf16[64,512]{1,0:T(8,128)(2,1)} %param.16) | copy-start | bytes 196612
  1.7 1.0 %copy-start = (bf16[64,8,512]{2,1,0:T(8,128)(2,1)S(1)}, bf16[64,8,512]{2,1,0:T(8,128)(2,1)}, u32[]{:S(2)}) copy-start(bf16[64,8,512]{2,1,0:T(8,128)(2,1)} %param.15) | copy-start | bytes 1572868
  1.9 0.9 copy-start.1
  1.9 0.9 copy-start.2
  1.9 0.9 copy-start.3
  1.9 0.9 copy-start.4
  1.9 0.9 copy-start.5

commit v3 on v2

--- a/solution.py
+++ b/solution.py
@@ -11,6 +11,7 @@
 NOPE = 128
 DV = 128
 CAP = 5
+PART = CAP + 1
 NDP = 32
 NH = 8
 MESH = pl.DeviceIdType.MESH
@@ -41,6 +42,10 @@
     )
 
 
+def settle(like, sem):
+    pltpu.make_async_copy(like, like, sem).wait()
+
+
 def dot_nt(a, b):
     return lax.dot_general(a, b, (((1,), (1,)), ((), ())), preferred_element_type=F32)
 
@@ -53,17 +58,18 @@
     dev_ref, block_ref, len_ref, freq_ref, pool_hbm, rope_hbm, kv_hbm, qn_hbm, qr_hbm,
     newl_ref, newr_ref, out_ref,
     pool_ref, rope_ref, kv_ref, kvf, wk_ref, wv_ref, qn_ref, qr_ref, fetch_sem,
-    req, tab, tabs, reqv, reqs, slat, srope, rlat, rrope, rropef, clat, crope, kmat, kr, wkf, wvf,
+    req, tab, tabs, reqv, reqs, slat, rlat0, rlat1, rropef, clat, crope, kmat, kr, wkf, wvf,
     qsend, qmat, osend, oall,
-    local_sem, req_ss, req_rs, lat_ss, lat_rs, rope_ss, rope_rs,
-    wk_ss, wk_rs, wv_ss, wv_rs, q_ss, q_rs, c_ss, c_rs, cr_ss, cr_rs, o_ss, o_rs,
+    local_sem, req_s, req_r, lat_s, lat_r, wk_ss, wk_rs, wv_ss, wv_rs,
+    q_s, q_r, c_s, c_r, cr_s, cr_r, o_s, o_r,
 ):
+    rlat = (rlat0, rlat1)
     me = lax.axis_index("dp")
     h = lax.axis_index("head")
     x, zh, c = me // 8, (me // 2) % 4, me % 2
 
     def dp_peer(o):
-        return ((x + o // 8) % 4) * 8 + ((zh + (o // 2) % 4) % 4) * 2 + (c + o % 2) % 2
+        return ((x + 4 - o // 8) % 4) * 8 + ((zh + 4 - (o // 2) % 4) % 4) * 2 + (c + o % 2) % 2
 
     zl, y = h // 4, h % 4
     flip = (1 - zl) * 4 + y
@@ -113,7 +119,7 @@
         found = jnp.sum(jnp.where(hit, blk, 0), axis=1, keepdims=True)
         asked = jnp.where(lanes == slot, found, asked)
     req[...] = asked.reshape(NDP, 1, 128)
-    tab[0:1, :] = dev * CAP + rank
+    tab[0:1, :] = dev * PART + rank
     tab[1:2, :] = dev * 8 + rank
     tab_copy = pltpu.make_async_copy(tab, tabs, local_sem.at[2])
     tab_copy.start()
@@ -163,104 +169,95 @@
 
     def req_copy(o):
         p = dp_peer(o)
-        return remote(req.at[p], reqv.at[me], req_ss.at[p], req_rs.at[me], (p, across(o)))
-
-    def req_arrival(o):
-        p = dp_peer(o)
-        return remote(req.at[p], reqv.at[p], req_ss.at[p], req_rs.at[p], (p, across(o)))
-
-    def z_dev(k):
+        return remote(req.at[p], reqv.at[me], req_s, req_r, (p, across(o)))
+
+    def along_z(k):
         return (x * 8 + ((zh + k) % 4) * 2 + c, h)
 
+    def along_x(k):
+        return (((x + k) % 4) * 8 + zh * 2 + c, h)
+
+    other_core = (x * 8 + zh * 2 + (1 - c), h)
+
     def z_copy(own, full, ss, rs, k):
-        return remote(own, full.at[x, zh, c], ss.at[k], rs.at[k], z_dev(k))
-
-    def z_arrival(own, full, ss, rs, k):
-        return remote(own, full.at[x, (zh + 4 - k) % 4, c], ss.at[k], rs.at[k], z_dev(k))
-
-    def z_relay(full, ss, rs, k):
-        part = full.at[x, (zh + 4 - k) % 4, c, pl.ds(0 if k == 1 else 8, 8)]
-        return remote(part, part, ss.at[8 + k], rs.at[8 + k], z_dev(k))
-
-    def z_relay_arrival(full, ss, rs, k):
-        part = full.at[x, (zh + 2) % 4, c, pl.ds(0 if k == 1 else 8, 8)]
-        return remote(part, part, ss.at[8 + k], rs.at[8 + k], z_dev(k))
-
-    def x_copy(full, ss, rs, k):
-        p = (((x + k) % 4) * 8 + zh * 2 + c, h)
-        return remote(full.at[x, :, c], full.at[x, :, c], ss.at[3 + k], rs.at[3 + k], p)
-
-    def x_arrival(full, ss, rs, k):
-        xx = (x + 4 - k) % 4
-        return remote(
-            full.at[xx, :, c], full.at[xx, :, c], ss.at[3 + k], rs.at[3 + k], (xx * 8 + zh * 2 + c, h)
-        )
-
-    def core_copy(full, ss, rs):
-        p = (x * 8 + zh * 2 + (1 - c), h)
-        return remote(full.at[:, :, c], full.at[:, :, c], ss.at[7], rs.at[7], p)
-
-    def core_arrival(full, ss, rs):
-        p = (x * 8 + zh * 2 + (1 - c), h)
-        return remote(full.at[:, :, 1 - c], full.at[:, :, 1 - c], ss.at[7], rs.at[7], p)
-
-    def z_stage(own, full, ss, rs, sem):
-        pltpu.make_async_copy(own, full.at[x, zh, c], sem).start()
+        return remote(own, full.at[x, zh, c], ss.at[0], rs.at[k // 2], along_z(k))
+
+    def z_own(own, full, sem):
+        return pltpu.make_async_copy(own, full.at[x, zh, c], sem)
+
+    def z_start(own, full, ss, rs, sem):
+        z_own(own, full, sem).start()
         for k in (1, 3):
             z_copy(own, full, ss, rs, k).start()
 
     def z_pass(own, full, ss, rs):
         for k in (1, 3):
-            z_arrival(own, full, ss, rs, k).wait_recv()
-            z_relay(full, ss, rs, k).start()
-
-    def x_stage(own, full, ss, rs, sem):
-        pltpu.make_async_copy(own, full.at[x, zh, c], sem).wait()
+            came = full.at[x, (zh + 4 - k) % 4, c]
+            remote(own, came, ss.at[0], rs.at[k // 2], along_z(k)).wait_recv()
+            part = full.at[x, (zh + 4 - k) % 4, c, pl.ds(0 if k == 1 else 8, 8)]
+            remote(part, part, ss.at[0], rs.at[2], along_z(k)).start()
+
+    def x_start(own, full, ss, rs, sem):
+        z_own(own, full, sem).wait()
+        settle(full.at[0, 0, 0], rs.at[2])
+        row = full.at[x, :, c]
         for k in (1, 3):
-            z_relay_arrival(full, ss, rs, k).wait_recv()
-        for k in (1, 2, 3):
-            x_copy(full, ss, rs, k).start()
-
-    def core_stage(full, ss, rs):
-        for k in (1, 2, 3):
-            x_arrival(full, ss, rs, k).wait_recv()
-        core_copy(full, ss, rs).start()
-
-    def weights_sent(own, full, ss, rs):
+            remote(row, row, ss.at[1], rs.at[3 + k // 2], along_x(k)).start()
+        remote(row, row, ss.at[2], rs.at[6], other_core).start()
+
+    def x_pass(full, ss, rs):
         for k in (1, 3):
-            z_copy(own, full, ss, rs, k).wait_send()
-            z_relay(full, ss, rs, k).wait_send()
-        for k in (1, 2, 3):
-            x_copy(full, ss, rs, k).wait_send()
-        core_copy(full, ss, rs).wait_send()
+            xx = (x + 4 - k) % 4
+            row = full.at[xx, :, c]
+            remote(row, row, ss.at[1], rs.at[3 + k // 2], along_x(k)).wait_recv()
+            part = full.at[xx, pl.ds(0 if k == 1 else 2, 2), c]
+            remote(part, part, ss.at[1], rs.at[5], along_x(k)).start()
+            remote(row, row, ss.at[2], rs.at[6], other_core).start()
+
+    def core_start(full, ss, rs):
+        settle(full.at[0, :, 0], rs.at[5])
+        row = full.at[(x + 2) % 4, :, c]
+        remote(row, row, ss.at[2], rs.at[6], other_core).start()
+
+    def core_arrival(full, rs):
+        settle(full.at[:, :, 0], rs.at[6])
+
+    def weights_sent(full, ss):
+        settle(full.at[0, pl.ds(0, 3), 0], ss.at[0])
+        settle(full.at[pl.ds(0, 3), :, 0], ss.at[1])
+        settle(full.at[:, :, 0], ss.at[2])
 
     @pl.loop(1, NDP)
     def _(o):
         req_copy(o).start()
 
-    z_stage(wk_ref, wkf, wk_ss, wk_rs, local_sem.at[0])
-    z_stage(wv_ref, wvf, wv_ss, wv_rs, local_sem.at[3])
+    z_start(wk_ref, wkf, wk_ss, wk_rs, local_sem.at[0])
+    z_start(wv_ref, wvf, wv_ss, wv_rs, local_sem.at[3])
     reqv[pl.ds(me, 1)] = req[pl.ds(me, 1)]
     z_pass(wk_ref, wkf, wk_ss, wk_rs)
     z_pass(wv_ref, wvf, wv_ss, wv_rs)
-
-    @pl.loop(1, NDP)
-    def _(o):
-        req_arrival(o).wait_recv()
+    settle(reqv.at[pl.ds(0, NDP - 1)], req_r)
 
     to_smem = pltpu.make_async_copy(reqv, reqs, local_sem.at[1])
     to_smem.start()
     to_smem.wait()
-    x_stage(wk_ref, wkf, wk_ss, wk_rs, local_sem.at[0])
+    x_start(wk_ref, wkf, wk_ss, wk_rs, local_sem.at[0])
     fetches[2].wait()
     fetches[3].wait()
 
     lane8 = lax.broadcasted_iota(jnp.int32, (8, 128), 1)
 
-    def gather(d, lat_dst, rope_dst):
+    def gather(d, own):
+        def put(at, value):
+            if own:
+                rlat0[at] = value[:16]
+                rlat1[at] = value[16:]
+            else:
+                slat[at] = value
+
         ids = [reqs[d, 0, s] for s in range(CAP)]
         for s in range(CAP):
-            lat_dst[CAP * d + s] = pool_ref[ids[s]]
+            put(PART * d + s, pool_ref[ids[s]])
         ropes = [rope_ref[ids[s]] for s in range(CAP)]
         rows = [
             jnp.where(lane8 < 64, ropes[0], ropes[1]),
@@ -268,37 +265,39 @@
             ropes[4],
             jnp.zeros((8, 128), F32),
         ]
-        rope_dst[d] = jnp.concatenate(rows, axis=0).astype(BF16)
-
-    def lat_copy(o):
+        put(PART * d + CAP, jnp.concatenate(rows, axis=0).astype(BF16))
+
+    def lat_copy(o, chunk):
         p = dp_peer(o)
-        part = pl.ds(CAP * p, CAP)
-        mine = pl.ds(CAP * me, CAP)
-        return remote(slat.at[part], rlat.at[mine], lat_ss.at[p], lat_rs.at[me], (p, across(o)))
-
-    def lat_arrival(o):
-        p = dp_peer(o)
-        part = pl.ds(CAP * p, CAP)
-        return remote(slat.at[part], rlat.at[part], lat_ss.at[p], lat_rs.at[p], (p, across(o)))
-
-    def rope_copy(o):
-        p = dp_peer(o)
-        return remote(srope.at[p], rrope.at[me], rope_ss.at[p], rope_rs.at[me], (p, across(o)))
-
-    def rope_arrival(o):
-        p = dp_peer(o)
-        return remote(srope.at[p], rrope.at[p], rope_ss.at[p], rope_rs.at[p], (p, across(o)))
-
-    @pl.loop(1, NDP)
+        rows = pl.ds(chunk * 16, 16)
+        return remote(
+            slat.at[pl.ds(PART * p, PART), rows],
+            rlat[chunk].at[pl.ds(PART * me, PART)],
+            lat_s.at[chunk],
+            lat_r.at[chunk],
+            (p, across(o)),
+        )
+
+    @pl.loop(1, 8)
     def _(o):
-        gather(dp_peer(o), slat, srope)
-        lat_copy(o).start()
-        rope_copy(o).start()
-
-    gather(me, rlat, rrope)
-
-    core_stage(wkf, wk_ss, wk_rs)
-    core_arrival(wkf, wk_ss, wk_rs).wait_recv()
+        gather(dp_peer(o), False)
+        lat_copy(o, 0).start()
+        lat_copy(o, 1).start()
+
+    x_pass(wkf, wk_ss, wk_rs)
+    @pl.loop(8, NDP)
+    def _(o):
+        gather(dp_peer(o), False)
+        lat_copy(o, 0).start()
+
+    core_start(wkf, wk_ss, wk_rs)
+    @pl.loop(8, NDP)
+    def _(o):
+        lat_copy(o, 1).start()
+
+    gather(me, True)
+
+    core_arrival(wkf, wk_rs)
 
     fetches[4].wait()
 
@@ -314,49 +313,27 @@
     def q_copy(k):
         p = head_peer(k)
         rows = pl.ds(h * 64, 64)
-        return remote(qsend.at[p // 2, p % 2], qmat.at[rows], q_ss.at[k], q_rs.at[k], (me, p))
-
-    def q_arrival(k):
-        p = head_from(k)
-        rows = pl.ds(p * 64, 64)
-        return remote(qsend.at[p // 2, p % 2], qmat.at[rows], q_ss.at[k], q_rs.at[k], (me, p))
+        return remote(qsend.at[p // 2, p % 2], qmat.at[rows], q_s, q_r, (me, p))
 
     for k in OTHERS:
         q_copy(k).start()
+    x_start(wv_ref, wvf, wv_ss, wv_rs, local_sem.at[3])
     q_own = pltpu.make_async_copy(
         qsend.at[h // 2, h % 2], qmat.at[pl.ds(h * 64, 64)], local_sem.at[4]
     )
     q_own.start()
 
-    x_stage(wv_ref, wvf, wv_ss, wv_rs, local_sem.at[3])
     tab_copy.wait()
 
-    @pl.loop(1, NDP)
-    def _(o):
-        lat_arrival(o).wait_recv()
-        rope_arrival(o).wait_recv()
-
-    @pl.loop(0, NDP)
-    def _(d):
-        rropef[pl.ds(4 * d, 4)] = rrope[d].astype(F32).reshape(4, 8, 128)
-
-    def c_copy(r, k):
+    def c_copy(r, chunk):
         rows = pl.ds(h * 64, 64)
-        return remote(clat.at[r], kmat.at[:, rows], c_ss.at[k], c_rs.at[k], (me, r))
-
-    def c_arrival(k):
-        p = head_from(k)
-        rows = pl.ds(p * 64, 64)
-        return remote(clat.at[p], kmat.at[:, rows], c_ss.at[k], c_rs.at[k], (me, p))
-
-    def cr_copy(r, k):
-        rows = pl.ds(h * 64, 64)
-        return remote(crope.at[r], kr.at[rows], cr_ss.at[k], cr_rs.at[k], (me, r))
-
-    def cr_arrival(k):
-        p = head_from(k)
-        rows = pl.ds(p * 64, 64)
-        return remote(crope.at[p], kr.at[rows], cr_ss.at[k], cr_rs.at[k], (me, p))
+        features = pl.ds(chunk * 256, 256)
+        return remote(
+            clat.at[chunk, r], kmat.at[:, rows, features], c_s.at[chunk], c_r.at[chunk], (me, r)
+        )
+
+    def cr_copy(r):
+        return remote(crope.at[r], kr.at[pl.ds(h * 64, 64)], cr_s, cr_r, (me, r))
 
     def side(entry, want):
         code = tabs[1, entry]
@@ -364,49 +341,87 @@
         turn = jnp.full((8, 128), code % 2, jnp.int32) != want
         return jnp.where(turn, pltpu.roll(value, 64, 1), value)
 
-    def compact(r):
+    def compact(r, chunk):
         for quarter in range(4):
             rows = pl.ds(quarter * 16, 16)
             for b in range(2):
                 entry = r * 16 + b * 8 + quarter * 2
-                first = rlat[tabs[0, entry]].astype(F32)
-                second = rlat[tabs[0, entry + 1]].astype(F32)
-                for j in range(4):
+                first = rlat[chunk][tabs[0, entry]].astype(F32)
+                second = rlat[chunk][tabs[0, entry + 1]].astype(F32)
+                for j in range(2):
                     tile = jnp.concatenate(
                         [first[8 * j : 8 * j + 8], second[8 * j : 8 * j + 8]], axis=0
                     )
-                    clat[r, b, rows, 128 * j : 128 * j + 128] = tile.astype(BF16)
+                    clat[chunk, r, b, rows, 128 * j : 128 * j + 128] = tile.astype(BF16)
+
+    def compact_rope(r):
+        for quarter in range(4):
+            rows = pl.ds(quarter * 16, 16)
             ropes = []
             for one in range(2):
                 entry = r * 16 + quarter * 2 + one
                 ropes.append(jnp.where(lane8 < 64, side(entry, 0), side(entry + 8, 1)))
             crope[r, rows, :] = jnp.concatenate(ropes, axis=0).astype(BF16)
 
+    own_rows = pl.ds(h * 64, 64)
+
+    def c_own(chunk):
+        return pltpu.make_async_copy(
+            clat.at[chunk, h],
+            kmat.at[:, own_rows, pl.ds(chunk * 256, 256)],
+            local_sem.at[5 + chunk],
+        )
+
+    cr_own = pltpu.make_async_copy(crope.at[h], kr.at[own_rows], local_sem.at[1])
+
+    settle(slat.at[pl.ds(0, PART * (NDP - 1)), pl.ds(0, 16)], lat_r.at[0])
+
     @pl.loop(0, NH)
     def _(k):
+        r = head_peer(k)
+        compact(r, 0)
+
         @pl.when(k != 4)
         def _():
-            r = head_peer(k)
-            compact(r)
-            c_copy(r, k).start()
-            cr_copy(r, k).start()
-
-    compact(h)
-    own_rows = pl.ds(h * 64, 64)
-    c_own = pltpu.make_async_copy(clat.at[h], kmat.at[:, own_rows], local_sem.at[5])
-    cr_own = pltpu.make_async_copy(crope.at[h], kr.at[own_rows], local_sem.at[6])
-    c_own.start()
+            c_copy(r, 0).start()
+
+    c_own(0).start()
+    x_pass(wvf, wv_ss, wv_rs)
+
+    settle(slat.at[pl.ds(0, PART * (NDP - 1)), pl.ds(0, 16)], lat_r.at[1])
+
+    @pl.loop(0, NDP)
+    def _(d):
+        ropes = [rlat0[PART * d + CAP].astype(F32), rlat1[PART * d + CAP].astype(F32)]
+        rropef[pl.ds(4 * d, 4)] = jnp.concatenate(ropes, axis=0).reshape(4, 8, 128)
+
+    @pl.loop(0, NH)
+    def _(k):
+        r = head_peer(k)
+        compact(r, 1)
+        compact_rope(r)
+
+        @pl.when(k != 4)
+        def _():
+            c_copy(r, 1).start()
+            cr_copy(r).start()
+
+    c_own(1).start()
     cr_own.start()
-    core_stage(wvf, wv_ss, wv_rs)
+    core_start(wvf, wv_ss, wv_rs)
+
+    settle(req.at[pl.ds(0, NDP - 1)], req_s)
+    for chunk in range(2):
+        settle(slat.at[pl.ds(0, PART * (NDP - 1)), pl.ds(0, 16)], lat_s.at[chunk])
 
     q_own.wait()
-    for k in OTHERS:
-        q_arrival(k).wait_recv()
-    c_own.wait()
+    settle(qmat.at[pl.ds(0, 448)], q_r)
+    settle(qmat.at[pl.ds(0, 448)], q_s)
+    for chunk in range(2):
+        c_own(chunk).wait()
+        settle(kmat.at[:, pl.ds(0, 448), pl.ds(0, 256)], c_r.at[chunk])
     cr_own.wait()
-    for k in OTHERS:
-        c_arrival(k).wait_recv()
-        cr_arrival(k).wait_recv()
+    settle(kr.at[pl.ds(0, 448)], cr_r)
 
     length = len_ref[h]
     newl = jnp.concatenate([newl_ref[h], jnp.zeros((112, LAT), BF16)], axis=0)
@@ -427,15 +442,8 @@
         tokens.append((of_entry + 8 * b) * 64 + part * 8 + column % 8)
     neg = -jnp.inf
 
-    def o_copy(p, k):
-        return remote(osend.at[pl.ds(p * 64, 64)], oall.at[h], o_ss.at[k], o_rs.at[k], (me, p))
-
-    def o_arrival(k):
-        p = head_from(k)
-        return remote(osend.at[pl.ds(p * 64, 64)], oall.at[p], o_ss.at[k], o_rs.at[k], (me, p))
-
-    def step_to(p):
-        return ((p // 4 + zl + 1) % 2) * 4 + (p + 4 - y) % 4
+    def o_copy(p):
+        return remote(osend.at[pl.ds(p * 64, 64)], oall.at[h], o_s, o_r, (me, p))
 
     def attend(block):
         rows = pl.ds(pl.multiple_of(block * 128, 128), 128)
@@ -472,16 +480,20 @@
         attend(block)
         for one in range(2):
             p = 2 * block + one
-            o_copy(p, step_to(p)).start()
+            o_copy(p).start()
 
     attend(h // 2)
     partner = 2 * (h // 2) + 1 - h % 2
-    o_copy(partner, step_to(partner)).start()
+    o_copy(partner).start()
     oall[pl.ds(h, 1)] = osend[pl.ds(pl.multiple_of(h * 64, 64), 64), :].reshape(1, 64, LAT)
 
-    core_arrival(wvf, wv_ss, wv_rs).wait_recv()
-    for k in OTHERS:
-        o_arrival(k).wait_recv()
+    core_arrival(wvf, wv_rs)
+    weights_sent(wkf, wk_ss)
+    weights_sent(wvf, wv_ss)
+    for chunk in range(2):
+        settle(kmat.at[:, pl.ds(0, 448), pl.ds(0, 256)], c_s.at[chunk])
+    settle(kr.at[pl.ds(0, 448)], cr_s)
+    settle(oall.at[pl.ds(0, 7)], o_r)
 
     first4 = lax.broadcasted_iota(jnp.int32, (4, 8, LAT), 1) < 4
     for quad in range(4):
@@ -498,19 +510,7 @@
                 result = dot_nn(value.reshape(32, LAT).astype(BF16), weight)
                 out_ref[:, g * DV : (g + 1) * DV] = result.astype(BF16)
 
-    @pl.loop(1, NDP)
-    def _(o):
-        req_copy(o).wait_send()
-        lat_copy(o).wait_send()
-        rope_copy(o).wait_send()
-
-    weights_sent(wk_ref, wkf, wk_ss, wk_rs)
-    weights_sent(wv_ref, wvf, wv_ss, wv_rs)
-    for k in OTHERS:
-        q_copy(k).wait_send()
-        c_copy(head_peer(k), k).wait_send()
-        cr_copy(head_peer(k), k).wait_send()
-        o_copy(head_peer(k), k).wait_send()
+    settle(oall.at[pl.ds(0, 7)], o_s)
 
 
 def per_device(
@@ -559,12 +559,11 @@
             pltpu.SMEM((8, 128), jnp.int32),
             pltpu.VMEM((NDP, 1, 128), jnp.int32),
             pltpu.SMEM((NDP, 1, 128), jnp.int32),
-            pltpu.VMEM((NDP * CAP, 32, 128), BF16),
-            pltpu.VMEM((NDP, 32, 128), BF16),
-            pltpu.VMEM((NDP * CAP, 32, 128), BF16),
-            pltpu.VMEM((NDP, 32, 128), BF16),
+            pltpu.VMEM((NDP * PART, 32, 128), BF16),
+            pltpu.VMEM((NDP * PART, 16, 128), BF16),
+            pltpu.VMEM((NDP * PART, 16, 128), BF16),
             pltpu.VMEM((NDP * 4, 8, 128), F32),
-            pltpu.VMEM((NH, 2, 64, LAT), BF16),
+            pltpu.VMEM((2, NH, 2, 64, LAT // 2), BF16),
             pltpu.VMEM((NH, 64, 128), BF16),
             pltpu.VMEM((2, 512, LAT), BF16),
             pltpu.VMEM((512, 128), BF16),
@@ -575,10 +574,9 @@
             pltpu.VMEM((512, LAT), BF16),
             pltpu.VMEM((NH, 64, LAT), BF16),
             dma((7,)),
-            dma((NDP,)), dma((NDP,)), dma((NDP,)), dma((NDP,)), dma((NDP,)), dma((NDP,)),
-            dma((12,)), dma((12,)), dma((12,)), dma((12,)),
-            dma((NH,)), dma((NH,)), dma((NH,)), dma((NH,)),
-            dma((NH,)), dma((NH,)), dma((NH,)), dma((NH,)),
+            dma, dma, dma((2,)), dma((2,)),
+            dma((3,)), dma((7,)), dma((3,)), dma((7,)),
+            dma, dma, dma((2,)), dma((2,)), dma, dma, dma, dma,
         ],
         compiler_params=pltpu.CompilerParams(
             collective_id=0, has_side_effects=True, vmem_limit_bytes=48 << 20

time: 96.4 us -> 88.3 us (0.916)
  Pallas kernels: 92.7 us -> 84.6 us
    pallas_call x1, Pallas kernels: 92.7 us -> 84.6 us  [per_device(): pl.pallas_call(kernel, out_shape=jax.ShapeDtypeStruct((requests * steps,...]
where the time goes in v3:
time: 88.3 us; the launch traced here: 88.1 us
  Pallas kernels  84.6 us (96%)
  local copies, waits for them, and re-layouts  2.61 us (3%)
    pallas_call x1, Pallas kernels, per_device(): pl.pallas_call(kernel, out_shape=jax.ShapeDtypeStruct((requests * steps,...  84.6 us

profile of v3, /device:TPU:1, one launch (start us, length us, event | category | flops | bytes accessed | tf_op | source)
XLA Modules:
  0.0 88.1 jit_solution(16124262501866985377)
XLA Ops:
  0.0 0.0 copy-start.6
  0.0 0.7 pad_convert_fusion.newr_ref
  0.7 0.0 copy-start.8
  0.7 0.0 copy-start.7
  0.8 0.9 %reshape.29.qr_hbm = bf16[32,1024]{1,0:T(8,128)(2,1)S(1)} reshape(bf16[8,4,1024]{2,1,0:T(4,128)(2,1)} %param.12) | data formatting | bytes 131072 | tf_op jit(solution)/shard_map/reshape | solution.py:533
  1.6 0.0 copy-done.6
  1.7 0.0 copy-start
  1.7 0.0 copy-done.8
  1.7 0.0 copy-done.7
  1.8 0.1 convert_element_type.9
  1.9 0.0 copy-start.1
  1.9 0.0 copy-start.2
  1.9 0.0 copy-start.3
  1.9 0.0 copy-start.4
  1.9 0.0 copy-start.5
  1.9 0.1 maximum_convert_fusion.rope_hbm
  2.1 0.6 copy-done
  2.7 0.1 copy-done.1
  2.8 0.0 copy-done.2
  2.8 0.0 copy-done.3
  2.8 0.0 copy-done.4
  2.8 0.0 copy-done.5
  2.8 84.6 %shard_map.109 = bf16[32,2048]{1,0:T(8,128)(2,1)S(1)} custom-call(s32[1,128]{1,0:T(1,128)S(1)} %bitcast.8, s32[1,128]{1,0:T(1,128)S(1)} %bitcast.9, s32[8]{0:T(128)S(1)} %copy-done.4, f32[1,128]{1,0:T(1,128)S(1)} %copy-done.5, bf16[64,32,128]{2,1,0:T(8,128)(2,1)S(1)} %bitcast.7, f32[64,8,128]{2,1,0:T(8,128)S(1)} %maximum_convert_fusion.rope_hbm, ...), custom_call_target="tpu_custom_call" | custom-call | tf_op jit(solution)/shard_map/pallas_call | solution.py:542
  87.4 0.7 reshape.30
  (2 shorter events, 0.1 us)
Async XLA Ops:
  0.0 1.6 %copy-start.6 = (bf16[8,4,2048]{2,1,0:T(4,128)(2,1)S(1)}, bf16[8,4,2048]{2,1,0:T(4,128)(2,1)}, u32[]{:S(2)}) copy-start(bf16[8,4,2048]{2,1,0:T(4,128)(2,1)} %param.11) | copy-start | bytes 393220
  0.7 1.0 %copy-start.8 = (bf16[8,4,512]{2,1,0:T(4,128)(2,1)S(1)}, bf16[8,4,512]{2,1,0:T(4,128)(2,1)}, u32[]{:S(2)}) copy-start(bf16[8,4,512]{2,1,0:T(4,128)(2,1)} %param.13) | copy-start | bytes 98308
  0.7 1.0 %copy-start.7 = (bf16[64,512]{1,0:T(8,128)(2,1)S(1)}, bf16[64,512]{1,0:T(8,128)(2,1)}, u32[]{:S(2)}) copy-start(bf16[64,512]{1,0:T(8,128)(2,1)} %param.16) | copy-start | bytes 196612
  1.7 1.0 %copy-start = (bf16[64,8,512]{2,1,0:T(8,128)(2,1)S(1)}, bf16[64,8,512]{2,1,0:T(8,128)(2,1)}, u32[]{:S(2)}) copy-start(bf16[64,8,512]{2,1,0:T(8,128)(2,1)} %param.15) | copy-start | bytes 1572868
  1.9 0.9 %copy-start.1 = (bf16[16,16,256]{2,1,0:T(8,128)(2,1)S(1)}, bf16[16,16,256]{2,1,0:T(8,128)(2,1)}, u32[]{:S(2)}) copy-start(bf16[16,16,256]{2,1,0:T(8,128)(2,1)} %kv_hbm.1) | copy-start | bytes 393220
  1.9 0.9 %copy-start.2 = (s32[128,1]{0,1:T(1,128)S(1)}, s32[128,1]{0,1:T(1,128)}, u32[]{:S(2)}) copy-start(s32[128,1]{0,1:T(1,128)} %param.18) | copy-start | bytes 1540
  1.9 0.9 %copy-start.3 = (s32[128]{0:T(128)S(1)}, s32[128]{0:T(128)}, u32[]{:S(2)}) copy-start(s32[128]{0:T(128)} %param.19) | copy-start | bytes 1540
  1.9 0.9 %copy-start.4 = (s32[8]{0:T(128)S(1)}, s32[8]{0:T(128)}, u32[]{:S(2)}) copy-start(s32[8]{0:T(128)} %len_ref.1) | copy-start | bytes 100
  1.9 0.9 %copy-start.5 = (f32[1,128]{1,0:T(1,128)S(1)}, f32[1,128]{1,0:T(1,128)}, u32[]{:S(2)}) copy-start(f32[1,128]{1,0:T(1,128)} %constant.7.clone.freq_ref) | copy-start | bytes 1540

commit v4 on v3

--- a/solution.py
+++ b/solution.py
@@ -75,6 +75,8 @@
     flip = (1 - zl) * 4 + y
 
     def across(o):
+        if isinstance(o, int):
+            return flip if (o // 2) % 4 == 2 else h
         return jnp.where((o // 2) % 4 == 2, flip, h)
 
     def head_peer(k):
@@ -91,8 +93,7 @@
 
     barrier = pltpu.get_barrier_semaphore()
 
-    @pl.loop(1, NDP)
-    def _(o):
+    for o in range(1, NDP):
         pl.semaphore_signal(
             barrier, inc=1, device_id=(dp_peer(o), across(o)), device_id_type=MESH
         )
@@ -227,8 +228,7 @@
         settle(full.at[pl.ds(0, 3), :, 0], ss.at[1])
         settle(full.at[:, :, 0], ss.at[2])
 
-    @pl.loop(1, NDP)
-    def _(o):
+    for o in range(1, NDP):
         req_copy(o).start()
 
     z_start(wk_ref, wkf, wk_ss, wk_rs, local_sem.at[0])
@@ -284,12 +284,12 @@
         lat_copy(o, 0).start()
         lat_copy(o, 1).start()
 
-    x_pass(wkf, wk_ss, wk_rs)
     @pl.loop(8, NDP)
     def _(o):
         gather(dp_peer(o), False)
         lat_copy(o, 0).start()
 
+    x_pass(wkf, wk_ss, wk_rs)
     core_start(wkf, wk_ss, wk_rs)
     @pl.loop(8, NDP)
     def _(o):

time: 88.3 us -> 87.5 us (level)
  Pallas kernels: 84.6 us -> 83.4 us
    pallas_call x1, Pallas kernels: 84.6 us -> 83.4 us  [per_device(): pl.pallas_call(kernel, out_shape=jax.ShapeDtypeStruct((requests * steps,...]
where the time goes in v4:
time: 87.5 us; the launch traced here: 87 us
  Pallas kernels  83.4 us (95%)
  local copies, waits for them, and re-layouts  2.61 us (3%)
    pallas_call x1, Pallas kernels, per_device(): pl.pallas_call(kernel, out_shape=jax.ShapeDtypeStruct((requests * steps,...  83.4 us

profile of v4, /device:TPU:1, one launch (start us, length us, event | category | flops | bytes accessed | tf_op | source)
XLA Modules:
  0.0 87.0 jit_solution(11317922099314811891)
XLA Ops:
  0.0 0.0 copy-start.6
  0.0 0.7 pad_convert_fusion.newr_ref
  0.7 0.0 copy-start.8
  0.7 0.0 copy-start.7
  0.8 0.9 %reshape.29.qr_hbm = bf16[32,1024]{1,0:T(8,128)(2,1)S(1)} reshape(bf16[8,4,1024]{2,1,0:T(4,128)(2,1)} %param.12) | data formatting | bytes 131072 | tf_op jit(solution)/shard_map/reshape | solution.py:533
  1.6 0.0 copy-done.6
  1.7 0.0 copy-start
  1.7 0.0 copy-done.8
  1.7 0.0 copy-done.7
  1.8 0.1 convert_element_type.9
  1.9 0.0 copy-start.1
  1.9 0.0 copy-start.2
  1.9 0.0 copy-start.3
  1.9 0.0 copy-start.4
  1.9 0.0 copy-start.5
  1.9 0.1 maximum_convert_fusion.rope_hbm
  2.1 0.6 copy-done
  2.7 0.1 copy-done.1
  2.8 0.0 copy-done.2
  2.8 0.0 copy-done.3
  2.8 0.0 copy-done.4
  2.8 0.0 copy-done.5
  2.8 83.4 %shard_map.109 = bf16[32,2048]{1,0:T(8,128)(2,1)S(1)} custom-call(s32[1,128]{1,0:T(1,128)S(1)} %bitcast.8, s32[1,128]{1,0:T(1,128)S(1)} %bitcast.9, s32[8]{0:T(128)S(1)} %copy-done.4, f32[1,128]{1,0:T(1,128)S(1)} %copy-done.5, bf16[64,32,128]{2,1,0:T(8,128)(2,1)S(1)} %bitcast.7, f32[64,8,128]{2,1,0:T(8,128)S(1)} %maximum_convert_fusion.rope_hbm, ...), custom_call_target="tpu_custom_call" | custom-call | tf_op jit(solution)/shard_map/pallas_call | solution.py:542
  86.3 0.7 reshape.30
  (2 shorter events, 0.1 us)
Async XLA Ops:
  0.0 1.6 %copy-start.6 = (bf16[8,4,2048]{2,1,0:T(4,128)(2,1)S(1)}, bf16[8,4,2048]{2,1,0:T(4,128)(2,1)}, u32[]{:S(2)}) copy-start(bf16[8,4,2048]{2,1,0:T(4,128)(2,1)} %param.11) | copy-start | bytes 393220
  0.7 1.0 %copy-start.8 = (bf16[8,4,512]{2,1,0:T(4,128)(2,1)S(1)}, bf16[8,4,512]{2,1,0:T(4,128)(2,1)}, u32[]{:S(2)}) copy-start(bf16[8,4,512]{2,1,0:T(4,128)(2,1)} %param.13) | copy-start | bytes 98308
  0.7 1.0 %copy-start.7 = (bf16[64,512]{1,0:T(8,128)(2,1)S(1)}, bf16[64,512]{1,0:T(8,128)(2,1)}, u32[]{:S(2)}) copy-start(bf16[64,512]{1,0:T(8,128)(2,1)} %param.16) | copy-start | bytes 196612
  1.7 1.0 %copy-start = (bf16[64,8,512]{2,1,0:T(8,128)(2,1)S(1)}, bf16[64,8,512]{2,1,0:T(8,128)(2,1)}, u32[]{:S(2)}) copy-start(bf16[64,8,512]{2,1,0:T(8,128)(2,1)} %param.15) | copy-start | bytes 1572868
  1.9 0.9 %copy-start.1 = (bf16[16,16,256]{2,1,0:T(8,128)(2,1)S(1)}, bf16[16,16,256]{2,1,0:T(8,128)(2,1)}, u32[]{:S(2)}) copy-start(bf16[16,16,256]{2,1,0:T(8,128)(2,1)} %kv_hbm.1) | copy-start | bytes 393220
  1.9 0.9 %copy-start.2 = (s32[128,1]{0,1:T(1,128)S(1)}, s32[128,1]{0,1:T(1,128)}, u32[]{:S(2)}) copy-start(s32[128,1]{0,1:T(1,128)} %param.18) | copy-start | bytes 1540
  1.9 0.9 %copy-start.3 = (s32[128]{0:T(128)S(1)}, s32[128]{0:T(128)}, u32[]{:S(2)}) copy-start(s32[128]{0:T(128)} %param.19) | copy-start | bytes 1540
  1.9 0.9 %copy-start.4 = (s32[8]{0:T(128)S(1)}, s32[8]{0:T(128)}, u32[]{:S(2)}) copy-start(s32[8]{0:T(128)} %len_ref.1) | copy-start | bytes 100
  1.9 0.9 %copy-start.5 = (f32[1,128]{1,0:T(1,128)S(1)}, f32[1,128]{1,0:T(1,128)}, u32[]{:S(2)}) copy-start(f32[1,128]{1,0:T(1,128)} %constant.7.clone.freq_ref) | copy-start | bytes 1540

commit v5 on v3

--- a/solution.py
+++ b/solution.py
@@ -75,6 +75,8 @@
     flip = (1 - zl) * 4 + y
 
     def across(o):
+        if isinstance(o, int):
+            return flip if (o // 2) % 4 == 2 else h
         return jnp.where((o // 2) % 4 == 2, flip, h)
 
     def head_peer(k):
@@ -278,22 +280,23 @@
             (p, across(o)),
         )
 
-    @pl.loop(1, 8)
-    def _(o):
-        gather(dp_peer(o), False)
-        lat_copy(o, 0).start()
-        lat_copy(o, 1).start()
-
+    near = (1, 8, 9, 16, 17, 24, 25)
+    far = tuple(o for o in range(8, NDP) if (o // 2) % 4)
+
+    def issue(steps, chunks):
+        for o in steps:
+            if 0 in chunks:
+                gather(dp_peer(o), False)
+            for chunk in chunks:
+                lat_copy(o, chunk).start()
+
+    issue(range(2, 8), (0, 1))
+    issue(far, (0,))
     x_pass(wkf, wk_ss, wk_rs)
-    @pl.loop(8, NDP)
-    def _(o):
-        gather(dp_peer(o), False)
-        lat_copy(o, 0).start()
-
+    issue(near, (0,))
     core_start(wkf, wk_ss, wk_rs)
-    @pl.loop(8, NDP)
-    def _(o):
-        lat_copy(o, 1).start()
+    issue(far, (1,))
+    issue(near, (1,))
 
     gather(me, True)
 

time: 88.3 us -> 87.7 us (level)
  Pallas kernels: 84.6 us -> 83.7 us
where the time goes in v5:
time: 87.7 us; the launch traced here: 87.3 us
  Pallas kernels  83.7 us (95%)
  local copies, waits for them, and re-layouts  2.61 us (3%)
    pallas_call x1, Pallas kernels, per_device(): pl.pallas_call(kernel, out_shape=jax.ShapeDtypeStruct((requests * steps,...  83.7 us

profile of v5, /device:TPU:1, one launch (start us, length us, event | category | flops | bytes accessed | tf_op | source)
XLA Modules:
  0.0 87.3 jit_solution(5596144397784179515)
XLA Ops:
  0.0 0.0 copy-start.6
  0.0 0.7 pad_convert_fusion.newr_ref
  0.7 0.0 copy-start.8
  0.7 0.0 copy-start.7
  0.8 0.9 %reshape.29.qr_hbm = bf16[32,1024]{1,0:T(8,128)(2,1)S(1)} reshape(bf16[8,4,1024]{2,1,0:T(4,128)(2,1)} %param.12) | data formatting | bytes 131072 | tf_op jit(solution)/shard_map/reshape | solution.py:536
  1.6 0.0 copy-done.6
  1.7 0.0 copy-start
  1.7 0.0 copy-done.8
  1.7 0.0 copy-done.7
  1.8 0.1 convert_element_type.9
  1.9 0.0 copy-start.1
  1.9 0.0 copy-start.2
  1.9 0.0 copy-start.3
  1.9 0.0 copy-start.4
  1.9 0.0 copy-start.5
  1.9 0.1 maximum_convert_fusion.rope_hbm
  2.1 0.6 copy-done
  2.7 0.1 copy-done.1
  2.8 0.0 copy-done.2
  2.8 0.0 copy-done.3
  2.8 0.0 copy-done.4
  2.8 0.0 copy-done.5
  2.8 83.7 %shard_map.109 = bf16[32,2048]{1,0:T(8,128)(2,1)S(1)} custom-call(s32[1,128]{1,0:T(1,128)S(1)} %bitcast.8, s32[1,128]{1,0:T(1,128)S(1)} %bitcast.9, s32[8]{0:T(128)S(1)} %copy-done.4, f32[1,128]{1,0:T(1,128)S(1)} %copy-done.5, bf16[64,32,128]{2,1,0:T(8,128)(2,1)S(1)} %bitcast.7, f32[64,8,128]{2,1,0:T(8,128)S(1)} %maximum_convert_fusion.rope_hbm, ...), custom_call_target="tpu_custom_call" | custom-call | tf_op jit(solution)/shard_map/pallas_call | solution.py:545
  86.5 0.7 reshape.30
  (2 shorter events, 0.1 us)
Async XLA Ops:
  0.0 1.6 %copy-start.6 = (bf16[8,4,2048]{2,1,0:T(4,128)(2,1)S(1)}, bf16[8,4,2048]{2,1,0:T(4,128)(2,1)}, u32[]{:S(2)}) copy-start(bf16[8,4,2048]{2,1,0:T(4,128)(2,1)} %param.11) | copy-start | bytes 393220
  0.7 1.0 %copy-start.8 = (bf16[8,4,512]{2,1,0:T(4,128)(2,1)S(1)}, bf16[8,4,512]{2,1,0:T(4,128)(2,1)}, u32[]{:S(2)}) copy-start(bf16[8,4,512]{2,1,0:T(4,128)(2,1)} %param.13) | copy-start | bytes 98308
  0.7 1.0 %copy-start.7 = (bf16[64,512]{1,0:T(8,128)(2,1)S(1)}, bf16[64,512]{1,0:T(8,128)(2,1)}, u32[]{:S(2)}) copy-start(bf16[64,512]{1,0:T(8,128)(2,1)} %param.16) | copy-start | bytes 196612
  1.7 1.0 %copy-start = (bf16[64,8,512]{2,1,0:T(8,128)(2,1)S(1)}, bf16[64,8,512]{2,1,0:T(8,128)(2,1)}, u32[]{:S(2)}) copy-start(bf16[64,8,512]{2,1,0:T(8,128)(2,1)} %param.15) | copy-start | bytes 1572868
  1.9 0.9 %copy-start.1 = (bf16[16,16,256]{2,1,0:T(8,128)(2,1)S(1)}, bf16[16,16,256]{2,1,0:T(8,128)(2,1)}, u32[]{:S(2)}) copy-start(bf16[16,16,256]{2,1,0:T(8,128)(2,1)} %kv_hbm.1) | copy-start | bytes 393220
  1.9 0.9 %copy-start.2 = (s32[128,1]{0,1:T(1,128)S(1)}, s32[128,1]{0,1:T(1,128)}, u32[]{:S(2)}) copy-start(s32[128,1]{0,1:T(1,128)} %param.18) | copy-start | bytes 1540
  1.9 0.9 %copy-start.3 = (s32[128]{0:T(128)S(1)}, s32[128]{0:T(128)}, u32[]{:S(2)}) copy-start(s32[128]{0:T(128)} %param.19) | copy-start | bytes 1540
  1.9 0.9 %copy-start.4 = (s32[8]{0:T(128)S(1)}, s32[8]{0:T(128)}, u32[]{:S(2)}) copy-start(s32[8]{0:T(128)} %len_ref.1) | copy-start | bytes 100
  1.9 0.9 %copy-start.5 = (f32[1,128]{1,0:T(1,128)S(1)}, f32[1,128]{1,0:T(1,128)}, u32[]{:S(2)}) copy-start(f32[1,128]{1,0:T(1,128)} %constant.7.clone.freq_ref) | copy-start | bytes 1540
